TPU v7x, 256 devices: a whole 4x4x8 slice. The times are simulated.
256 devices in a mesh: dp: 256 (over x, z, y, core).
Axes of the slice: x: 4, y: 4, z: 8, core: 2. Of those that a mesh axis runs over, the one named last changes fastest.
Arguments:
- image_embeds: bfloat16 [131072, 1152], P('dp'), may hold values from -6 to 6
- text_embeds: bfloat16 [131072, 1152], P('dp'), may hold values from -6 to 6
- logit_scale: float32 [1], replicated, may hold values from 0.02 to 0.06
- logit_bias: float32 [1], replicated, may hold values from -4 to -1
- plan: int32 [256, 6], P('dp'), may hold values from 0 to 255, as said below
Outputs:
- image_grad: float32 [131072, 1152], P('dp')
- text_grad: float32 [131072, 1152], P('dp')
- loss_tiles: float32 [256, 7], P('dp')
Inputs may be any that keep to these rules, and one draw needn't show every extreme that they name: In round r every block d meets plan[d, r] = d XOR (m_r * 32), where the round mask m_r lies in 1 to 7 and is the same for every d; the 6 masks differ from one another.
All inputs are finite; a program needn't handle non-finite values.
Results may differ from a plain program's by a relative error of at most 0.0028.
Values may be sent and summed in bfloat16 or wider, within the bound.
No kernel may reach another device: no remote copies, remote signals or barrier semaphores. Data moves between devices by JAX's collectives and lax.ppermute only.
A program may use at most 128 MiB of HBM per device.

v0:
```python
import jax
import jax.numpy as jnp
from jax import lax
from jax.sharding import PartitionSpec as P


def as_sent(x):

    def short(part):
        return part.astype(jnp.bfloat16) if part.dtype == jnp.float32 else part

    return jax.tree.map(short, x)


def from_partner(value, axis, stride):
    mask = 2**stride
    pairs = [(source, source ^ mask) for source in range(lax.axis_size(axis))]
    return lax.ppermute(value, axis, pairs)


def rows_by_rows(left, right):
    return lax.dot_general(
        left, right, (((1,), (1,)), ((), ())), preferred_element_type=jnp.float32
    )


def columns_by_columns(left, right):
    return lax.dot_general(
        left, right, (((0,), (0,)), ((), ())), preferred_element_type=jnp.float32
    )


def pair_tile(images, partner, logit_mult, logit_shift, label_sign):
    scores = rows_by_rows(images, partner)
    logits = logit_mult * scores + logit_shift
    tile_loss = jnp.mean(jax.nn.softplus(-label_sign * logits))
    coefficient = (-label_sign * jax.nn.sigmoid(-label_sign * logits) * logit_mult).astype(
        jnp.bfloat16
    )
    image_part = jnp.dot(coefficient, partner, preferred_element_type=jnp.float32)
    text_part = columns_by_columns(coefficient, images).astype(jnp.bfloat16)
    return (tile_loss, image_part, text_part)


def route_texts(moving, round_mask, low_bit, bit_order):

    def branch_for(mask_value):

        def carry_route(moving_block):
            for section_bit in bit_order:
                if mask_value >> section_bit & 1:
                    moving_block = jax.tree.map(
                        lambda part, own: part.astype(own.dtype),
                        from_partner(as_sent(moving_block), "dp", low_bit + section_bit),
                        moving_block,
                    )
            return moving_block

        return carry_route

    return lax.switch(
        round_mask - 1, [branch_for(mask_value) for mask_value in range(1, 8)], moving
    )


def route_grads(moving, round_mask, low_bit, bit_order):

    def branch_for(mask_value):

        def carry_route(moving_block):
            for section_bit in bit_order:
                if mask_value >> section_bit & 1:
                    moving_block = jax.tree.map(
                        lambda part, own: part.astype(own.dtype),
                        from_partner(as_sent(moving_block), "dp", low_bit + section_bit),
                        moving_block,
                    )
            return moving_block

        return carry_route

    return lax.switch(
        round_mask - 1, [branch_for(mask_value) for mask_value in range(1, 8)], moving
    )


def shards(image_embeds, text_embeds, logit_scale, logit_bias, plan):
    pair_rows = image_embeds.shape[0]
    round_count = plan.shape[1]
    low_bit = lax.axis_size("dp").bit_length() - 4
    my_index = lax.axis_index("dp")
    round_masks = jnp.right_shift(jnp.bitwise_xor(plan[0], my_index), low_bit)
    logit_mult = logit_scale[0]
    logit_shift = logit_bias[0]
    bit_order = (0, 1, 2)
    row_iota = lax.broadcasted_iota(jnp.int32, (pair_rows, pair_rows), 0)
    column_iota = lax.broadcasted_iota(jnp.int32, (pair_rows, pair_rows), 1)
    home_sign = jnp.where(row_iota == column_iota, 1.0, -1.0).astype(jnp.float32)
    away_sign = jnp.float32(-1.0)
    home_loss, image_grad, home_text = pair_tile(
        image_embeds, text_embeds, logit_mult, logit_shift, home_sign
    )
    text_grad = home_text.astype(jnp.float32)
    tile_losses = [home_loss]
    for round_no in range(round_count):
        round_mask = round_masks[round_no]
        partner = route_texts(text_embeds, round_mask, low_bit, bit_order)
        tile_loss, image_part, text_part = pair_tile(
            image_embeds, partner, logit_mult, logit_shift, away_sign
        )
        image_grad = image_grad + image_part
        returned = route_grads(text_part, round_mask, low_bit, bit_order)
        text_grad = text_grad + returned.astype(jnp.float32)
        tile_losses.append(tile_loss)
    return (image_grad, text_grad, jnp.stack(tile_losses).reshape(1, round_count + 1))


def solution(mesh):
    return jax.shard_map(
        shards,
        mesh=mesh,
        in_specs=(P("dp", None), P("dp", None), P(), P(), P("dp", None)),
        out_specs=(P("dp", None), P("dp", None), P("dp", None)),
        check_vma=False,
    )
```

profile of v0, /device:TPU:42, one launch (start us, length us, event | category | flops | bytes accessed | tf_op | source)
XLA Modules:
  0.0 664.8 jit_solution(11931904495179429599)
XLA Ops:
  11.1 86.5 %conditional.30 = (bf16[512,1152]{1,0:T(8,128)(2,1)}) conditional(s32[]{:T(128)} %bitcast.2, bf16[512,1152]{1,0:T(8,128)(2,1)S(1)} %copy-done.1, bf16[512,1152]{1,0:T(8,128)(2,1)S(1)} %copy-done.1, bf16[512,1152]{1,0:T(8,128)(2,1)S(1)} %copy-done.1, bf16[512,1152]{1,0:T(8,128)(2,1)S(1)} %copy-done.1, ...), branch_computations={%region_0.1_spmd, %region_1.2_spmd, %region_2.3_spmd, %region_3.4_... | conditional | bytes 14155904 | solution.py:61
  11.1 6.4 collective-permute-start.5
  17.5 51.5 %collective-permute-done.5 = bf16[512,1152]{1,0:T(8,128)(2,1)S(1)} collective-permute-done((bf16[512,1152]{1,0:T(8,128)(2,1)S(1)}, bf16[512,1152]{1,0:T(8,128)(2,1)S(1)}, u32[]{:S(2)}, u32[]{:S(2)}) %collective-permute-start.5) | collective-permute-done | bytes 1179680 | tf_op jit(solution)/shard_map/cond/branch_4_fun/ppermute | solution.py:18
  71.1 26.5 %collective-permute-done.6 = bf16[512,1152]{1,0:T(8,128)(2,1)} collective-permute-done((bf16[512,1152]{1,0:T(8,128)(2,1)S(1)}, bf16[512,1152]{1,0:T(8,128)(2,1)}, u32[]{:S(2)}, u32[]{:S(2)}) %collective-permute-start.6) | collective-permute-done | bytes 1179680 | tf_op jit(solution)/shard_map/cond/branch_4_fun/ppermute | solution.py:18
  105.6 27.9 %conditional.31 = (bf16[512,1152]{1,0:T(8,128)(2,1)}) conditional(s32[]{:T(128)} %bitcast.4, bf16[512,1152]{1,0:T(8,128)(2,1)S(1)} %copy-done.1, bf16[512,1152]{1,0:T(8,128)(2,1)S(1)} %copy-done.1, bf16[512,1152]{1,0:T(8,128)(2,1)S(1)} %copy-done.1, bf16[512,1152]{1,0:T(8,128)(2,1)S(1)} %copy-done.1, ...), branch_computations={%region_7.8_spmd, %region_8.9_spmd, %region_9.10_spmd, %region_10.... | conditional | bytes 14155904 | solution.py:61
  108.1 25.5 %collective-permute-done.16 = bf16[512,1152]{1,0:T(8,128)(2,1)} collective-permute-done((bf16[512,1152]{1,0:T(8,128)(2,1)S(1)}, bf16[512,1152]{1,0:T(8,128)(2,1)}, u32[]{:S(2)}, u32[]{:S(2)}) %collective-permute-start.16) | collective-permute-done | bytes 1179680 | tf_op jit(solution)/shard_map/cond/branch_3_fun/ppermute | solution.py:18
  141.8 76.8 %conditional.32 = (bf16[512,1152]{1,0:T(8,128)(2,1)}) conditional(s32[]{:T(128)} %bitcast.6, bf16[512,1152]{1,0:T(8,128)(2,1)S(1)} %copy-done.1, bf16[512,1152]{1,0:T(8,128)(2,1)S(1)} %copy-done.1, bf16[512,1152]{1,0:T(8,128)(2,1)S(1)} %copy-done.1, bf16[512,1152]{1,0:T(8,128)(2,1)S(1)} %copy-done.1, ...), branch_computations={%region_14.15_spmd, %region_15.16_spmd, %region_16.17_spmd, %regio... | conditional | bytes 14155904 | solution.py:61
  147.0 43.4 %collective-permute-done.26 = bf16[512,1152]{1,0:T(8,128)(2,1)S(1)} collective-permute-done((bf16[512,1152]{1,0:T(8,128)(2,1)S(1)}, bf16[512,1152]{1,0:T(8,128)(2,1)S(1)}, u32[]{:S(2)}, u32[]{:S(2)}) %collective-permute-start.26) | collective-permute-done | bytes 1179680 | tf_op jit(solution)/shard_map/cond/branch_2_fun/ppermute | solution.py:18
  190.8 27.5 %collective-permute-done.27 = bf16[512,1152]{1,0:T(8,128)(2,1)} collective-permute-done((bf16[512,1152]{1,0:T(8,128)(2,1)S(1)}, bf16[512,1152]{1,0:T(8,128)(2,1)}, u32[]{:S(2)}, u32[]{:S(2)}) %collective-permute-start.27) | collective-permute-done | bytes 1179680 | tf_op jit(solution)/shard_map/cond/branch_2_fun/ppermute | solution.py:18
  226.8 33.7 %conditional.33 = (bf16[512,1152]{1,0:T(8,128)(2,1)}) conditional(s32[]{:T(128)} %bitcast.8, bf16[512,1152]{1,0:T(8,128)(2,1)S(1)} %copy-done.1, bf16[512,1152]{1,0:T(8,128)(2,1)S(1)} %copy-done.1, bf16[512,1152]{1,0:T(8,128)(2,1)S(1)} %copy-done.1, bf16[512,1152]{1,0:T(8,128)(2,1)S(1)} %copy-done.1, ...), branch_computations={%region_21.22_spmd, %region_22.23_spmd, %region_23.24_spmd, %regio... | conditional | bytes 14155904 | solution.py:61
  232.3 28.2 %collective-permute-done.36 = bf16[512,1152]{1,0:T(8,128)(2,1)} collective-permute-done((bf16[512,1152]{1,0:T(8,128)(2,1)S(1)}, bf16[512,1152]{1,0:T(8,128)(2,1)}, u32[]{:S(2)}, u32[]{:S(2)}) %collective-permute-start.36) | collective-permute-done | bytes 1179680 | tf_op jit(solution)/shard_map/cond/branch_0_fun/ppermute | solution.py:18
  268.7 28.2 %conditional.34 = (bf16[512,1152]{1,0:T(8,128)(2,1)}) conditional(s32[]{:T(128)} %bitcast.10, bf16[512,1152]{1,0:T(8,128)(2,1)S(1)} %copy-done.1, bf16[512,1152]{1,0:T(8,128)(2,1)S(1)} %copy-done.1, bf16[512,1152]{1,0:T(8,128)(2,1)S(1)} %copy-done.1, bf16[512,1152]{1,0:T(8,128)(2,1)S(1)} %copy-done.1, ...), branch_computations={%region_28.29_spmd, %region_29.30_spmd, %region_30.31_spmd, %regio... | conditional | bytes 14155904 | solution.py:61
  269.2 27.5 %collective-permute-done.49 = bf16[512,1152]{1,0:T(8,128)(2,1)} collective-permute-done((bf16[512,1152]{1,0:T(8,128)(2,1)S(1)}, bf16[512,1152]{1,0:T(8,128)(2,1)}, u32[]{:S(2)}, u32[]{:S(2)}) %collective-permute-start.49) | collective-permute-done | bytes 1179680 | tf_op jit(solution)/shard_map/cond/branch_1_fun/ppermute | solution.py:18
  305.0 55.9 %conditional.35 = (bf16[512,1152]{1,0:T(8,128)(2,1)}) conditional(s32[]{:T(128)} %bitcast.12, bf16[512,1152]{1,0:T(8,128)(2,1)S(1)} %copy-done.1, bf16[512,1152]{1,0:T(8,128)(2,1)S(1)} %copy-done.1, bf16[512,1152]{1,0:T(8,128)(2,1)S(1)} %copy-done.1, bf16[512,1152]{1,0:T(8,128)(2,1)S(1)} %copy-done.1, ...), branch_computations={%region_35.36_spmd, %region_36.37_spmd, %region_37.38_spmd, %regio... | conditional | bytes 14155904 | solution.py:61
  305.6 26.5 %collective-permute-done.67 = bf16[512,1152]{1,0:T(8,128)(2,1)S(1)} collective-permute-done((bf16[512,1152]{1,0:T(8,128)(2,1)S(1)}, bf16[512,1152]{1,0:T(8,128)(2,1)S(1)}, u32[]{:S(2)}, u32[]{:S(2)}) %collective-permute-start.67) | collective-permute-done | bytes 1179680 | tf_op jit(solution)/shard_map/cond/branch_5_fun/ppermute | solution.py:18
  336.2 24.3 %collective-permute-done.68 = bf16[512,1152]{1,0:T(8,128)(2,1)} collective-permute-done((bf16[512,1152]{1,0:T(8,128)(2,1)S(1)}, bf16[512,1152]{1,0:T(8,128)(2,1)}, u32[]{:S(2)}, u32[]{:S(2)}) %collective-permute-start.68) | collective-permute-done | bytes 1179680 | tf_op jit(solution)/shard_map/cond/branch_5_fun/ppermute | solution.py:18
  370.8 53.0 %conditional.41 = (bf16[512,1152]{1,0:T(8,128)(2,1)}) conditional(s32[]{:T(128)} %bitcast.12, bf16[512,1152]{1,0:T(8,128)(2,1)S(1)} %convolution_convert_fusion, bf16[512,1152]{1,0:T(8,128)(2,1)S(1)} %convolution_convert_fusion, bf16[512,1152]{1,0:T(8,128)(2,1)S(1)} %convolution_convert_fusion, ...), branch_computations={%region_77.78_spmd, %region_78.79_spmd, %region_79.80_spmd, %regio... | conditional | bytes 14155904
  372.6 24.0 %collective-permute-done.139 = bf16[512,1152]{1,0:T(8,128)(2,1)S(1)} collective-permute-done((bf16[512,1152]{1,0:T(8,128)(2,1)S(1)}, bf16[512,1152]{1,0:T(8,128)(2,1)S(1)}, u32[]{:S(2)}, u32[]{:S(2)}) %collective-permute-start.139) | collective-permute-done | bytes 1179680 | tf_op jit(solution)/shard_map/cond/branch_5_fun/ppermute | solution.py:18
  399.6 24.3 %collective-permute-done.140 = bf16[512,1152]{1,0:T(8,128)(2,1)} collective-permute-done((bf16[512,1152]{1,0:T(8,128)(2,1)S(1)}, bf16[512,1152]{1,0:T(8,128)(2,1)}, u32[]{:S(2)}, u32[]{:S(2)}) %collective-permute-start.140) | collective-permute-done | bytes 1179680 | tf_op jit(solution)/shard_map/cond/branch_5_fun/ppermute | solution.py:18
  426.1 25.1 %conditional.40 = (bf16[512,1152]{1,0:T(8,128)(2,1)}) conditional(s32[]{:T(128)} %bitcast.10, bf16[512,1152]{1,0:T(8,128)(2,1)S(1)} %convolution_convert_fusion.1, bf16[512,1152]{1,0:T(8,128)(2,1)S(1)} %convolution_convert_fusion.1, bf16[512,1152]{1,0:T(8,128)(2,1)S(1)} %convolution_convert_fusion.1, ...), branch_computations={%region_70.71_spmd, %region_71.72_spmd, %region_72.73_spmd, %regio... | conditional | bytes 14155904
  427.5 23.5 %collective-permute-done.121 = bf16[512,1152]{1,0:T(8,128)(2,1)} collective-permute-done((bf16[512,1152]{1,0:T(8,128)(2,1)S(1)}, bf16[512,1152]{1,0:T(8,128)(2,1)}, u32[]{:S(2)}, u32[]{:S(2)}) %collective-permute-start.121) | collective-permute-done | bytes 1179680 | tf_op jit(solution)/shard_map/cond/branch_1_fun/ppermute | solution.py:18
  453.4 50.2 %conditional.39 = (bf16[512,1152]{1,0:T(8,128)(2,1)}) conditional(s32[]{:T(128)} %bitcast.8, bf16[512,1152]{1,0:T(8,128)(2,1)S(1)} %convolution_convert_fusion.2, bf16[512,1152]{1,0:T(8,128)(2,1)S(1)} %convolution_convert_fusion.2, bf16[512,1152]{1,0:T(8,128)(2,1)S(1)} %convolution_convert_fusion.2, ...), branch_computations={%region_63.64_spmd, %region_64.65_spmd, %region_65.66_spmd, %regio... | conditional | bytes 14155904
  453.4 6.0 collective-permute-start.108
  459.4 44.2 %collective-permute-done.108 = bf16[512,1152]{1,0:T(8,128)(2,1)} collective-permute-done((bf16[512,1152]{1,0:T(8,128)(2,1)S(1)}, bf16[512,1152]{1,0:T(8,128)(2,1)}, u32[]{:S(2)}, u32[]{:S(2)}) %collective-permute-start.108) | collective-permute-done | bytes 1179680 | tf_op jit(solution)/shard_map/cond/branch_0_fun/ppermute | solution.py:18
  505.8 59.3 %conditional.38 = (bf16[512,1152]{1,0:T(8,128)(2,1)}) conditional(s32[]{:T(128)} %bitcast.6, bf16[512,1152]{1,0:T(8,128)(2,1)S(1)} %convolution_convert_fusion.3, bf16[512,1152]{1,0:T(8,128)(2,1)S(1)} %convolution_convert_fusion.3, bf16[512,1152]{1,0:T(8,128)(2,1)S(1)} %convolution_convert_fusion.3, ...), branch_computations={%region_56.57_spmd, %region_57.58_spmd, %region_58.59_spmd, %regio... | conditional | bytes 14155904
  506.5 31.2 %collective-permute-done.98 = bf16[512,1152]{1,0:T(8,128)(2,1)S(1)} collective-permute-done((bf16[512,1152]{1,0:T(8,128)(2,1)S(1)}, bf16[512,1152]{1,0:T(8,128)(2,1)S(1)}, u32[]{:S(2)}, u32[]{:S(2)}) %collective-permute-start.98) | collective-permute-done | bytes 1179680 | tf_op jit(solution)/shard_map/cond/branch_2_fun/ppermute | solution.py:18
  538.0 26.8 %collective-permute-done.99 = bf16[512,1152]{1,0:T(8,128)(2,1)} collective-permute-done((bf16[512,1152]{1,0:T(8,128)(2,1)S(1)}, bf16[512,1152]{1,0:T(8,128)(2,1)}, u32[]{:S(2)}, u32[]{:S(2)}) %collective-permute-start.99) | collective-permute-done | bytes 1179680 | tf_op jit(solution)/shard_map/cond/branch_2_fun/ppermute | solution.py:18
  567.2 27.8 %conditional.37 = (bf16[512,1152]{1,0:T(8,128)(2,1)}) conditional(s32[]{:T(128)} %bitcast.4, bf16[512,1152]{1,0:T(8,128)(2,1)S(1)} %convolution_convert_fusion.4, bf16[512,1152]{1,0:T(8,128)(2,1)S(1)} %convolution_convert_fusion.4, bf16[512,1152]{1,0:T(8,128)(2,1)S(1)} %convolution_convert_fusion.4, ...), branch_computations={%region_49.50_spmd, %region_50.51_spmd, %region_51.52_spmd, %regio... | conditional | bytes 14155904
  567.4 27.7 %collective-permute-done.88 = bf16[512,1152]{1,0:T(8,128)(2,1)} collective-permute-done((bf16[512,1152]{1,0:T(8,128)(2,1)S(1)}, bf16[512,1152]{1,0:T(8,128)(2,1)}, u32[]{:S(2)}, u32[]{:S(2)}) %collective-permute-start.88) | collective-permute-done | bytes 1179680 | tf_op jit(solution)/shard_map/cond/branch_3_fun/ppermute | solution.py:18
  597.3 55.1 %conditional.36 = (bf16[512,1152]{1,0:T(8,128)(2,1)}) conditional(s32[]{:T(128)} %bitcast.2, bf16[512,1152]{1,0:T(8,128)(2,1)S(1)} %convolution_convert_fusion.5, bf16[512,1152]{1,0:T(8,128)(2,1)S(1)} %convolution_convert_fusion.5, bf16[512,1152]{1,0:T(8,128)(2,1)S(1)} %convolution_convert_fusion.5, ...), branch_computations={%region_42.43_spmd, %region_43.44_spmd, %region_44.45_spmd, %regio... | conditional | bytes 14155904
  597.5 29.0 %collective-permute-done.77 = bf16[512,1152]{1,0:T(8,128)(2,1)S(1)} collective-permute-done((bf16[512,1152]{1,0:T(8,128)(2,1)S(1)}, bf16[512,1152]{1,0:T(8,128)(2,1)S(1)}, u32[]{:S(2)}, u32[]{:S(2)}) %collective-permute-start.77) | collective-permute-done | bytes 1179680 | tf_op jit(solution)/shard_map/cond/branch_4_fun/ppermute | solution.py:18
  627.1 25.3 %collective-permute-done.78 = bf16[512,1152]{1,0:T(8,128)(2,1)} collective-permute-done((bf16[512,1152]{1,0:T(8,128)(2,1)S(1)}, bf16[512,1152]{1,0:T(8,128)(2,1)}, u32[]{:S(2)}, u32[]{:S(2)}) %collective-permute-start.78) | collective-permute-done | bytes 1179680 | tf_op jit(solution)/shard_map/cond/branch_4_fun/ppermute | solution.py:18
  (71 shorter events, 103.3 us)
Async XLA Ops:
  0.6 1.8 copy-start
  6.1 3.7 copy-start.2
  6.1 4.9 copy-start.1
  11.1 57.9 %collective-permute-start.5 = (bf16[512,1152]{1,0:T(8,128)(2,1)S(1)}, bf16[512,1152]{1,0:T(8,128)(2,1)S(1)}, u32[]{:S(2)}, u32[]{:S(2)}) collective-permute-start(bf16[512,1152]{1,0:T(8,128)(2,1)S(1)} %param.4), channel_id=1, source_target_pairs={{0,32},{1,33},{2,34},{3,35},{4,36},{5,37},{6,38},{7,39},{8,40},{9,... | collective-permute-start | bytes 3538952 | tf_op jit(solution)/shard_map/cond/branch_4_fun/ppermute | solution.py:18
  69.0 28.6 %collective-permute-start.6 = (bf16[512,1152]{1,0:T(8,128)(2,1)S(1)}, bf16[512,1152]{1,0:T(8,128)(2,1)}, u32[]{:S(2)}, u32[]{:S(2)}) collective-permute-start(bf16[512,1152]{1,0:T(8,128)(2,1)S(1)} %collective-permute-done.5), channel_id=1, source_target_pairs={{0,128},{1,129},{2,130},{3,131},{4,132},{5,133},{6,134},{7,135},{8... | collective-permute-start | bytes 3538952 | tf_op jit(solution)/shard_map/cond/branch_4_fun/ppermute | solution.py:18
  97.6 3.5 copy-start.3
  101.1 4.0 copy-start.8
  105.8 27.7 %collective-permute-start.16 = (bf16[512,1152]{1,0:T(8,128)(2,1)S(1)}, bf16[512,1152]{1,0:T(8,128)(2,1)}, u32[]{:S(2)}, u32[]{:S(2)}) collective-permute-start(bf16[512,1152]{1,0:T(8,128)(2,1)S(1)} %param.10), channel_id=1, source_target_pairs={{0,128},{1,129},{2,130},{3,131},{4,132},{5,133},{6,134},{7,135},{8... | collective-permute-start | bytes 3538952 | tf_op jit(solution)/shard_map/cond/branch_3_fun/ppermute | solution.py:18
  133.6 3.5 copy-start.4
  137.1 4.0 copy-start.9
  141.8 48.5 %collective-permute-start.26 = (bf16[512,1152]{1,0:T(8,128)(2,1)S(1)}, bf16[512,1152]{1,0:T(8,128)(2,1)S(1)}, u32[]{:S(2)}, u32[]{:S(2)}) collective-permute-start(bf16[512,1152]{1,0:T(8,128)(2,1)S(1)} %param.16), channel_id=1, source_target_pairs={{0,32},{1,33},{2,34},{3,35},{4,36},{5,37},{6,38},{7,39},{8,40},{9,... | collective-permute-start | bytes 3538952 | tf_op jit(solution)/shard_map/cond/branch_2_fun/ppermute | solution.py:18
  190.3 27.9 %collective-permute-start.27 = (bf16[512,1152]{1,0:T(8,128)(2,1)S(1)}, bf16[512,1152]{1,0:T(8,128)(2,1)}, u32[]{:S(2)}, u32[]{:S(2)}) collective-permute-start(bf16[512,1152]{1,0:T(8,128)(2,1)S(1)} %collective-permute-done.26), channel_id=1, source_target_pairs={{0,64},{1,65},{2,66},{3,67},{4,68},{5,69},{6,70},{7,71},{8,72},{9,... | collective-permute-start | bytes 3538952 | tf_op jit(solution)/shard_map/cond/branch_2_fun/ppermute | solution.py:18
  218.6 3.5 copy-start.5
  222.1 4.0 copy-start.10
  226.8 33.7 %collective-permute-start.36 = (bf16[512,1152]{1,0:T(8,128)(2,1)S(1)}, bf16[512,1152]{1,0:T(8,128)(2,1)}, u32[]{:S(2)}, u32[]{:S(2)}) collective-permute-start(bf16[512,1152]{1,0:T(8,128)(2,1)S(1)} %param.21), channel_id=1, source_target_pairs={{0,32},{1,33},{2,34},{3,35},{4,36},{5,37},{6,38},{7,39},{8,40},{9,... | collective-permute-start | bytes 3538952 | tf_op jit(solution)/shard_map/cond/branch_0_fun/ppermute | solution.py:18
  260.5 3.6 copy-start.6
  264.0 4.0 copy-start.11
  268.7 28.0 %collective-permute-start.49 = (bf16[512,1152]{1,0:T(8,128)(2,1)S(1)}, bf16[512,1152]{1,0:T(8,128)(2,1)}, u32[]{:S(2)}, u32[]{:S(2)}) collective-permute-start(bf16[512,1152]{1,0:T(8,128)(2,1)S(1)} %param.29), channel_id=1, source_target_pairs={{0,64},{1,65},{2,66},{3,67},{4,68},{5,69},{6,70},{7,71},{8,72},{9,... | collective-permute-start | bytes 3538952 | tf_op jit(solution)/shard_map/cond/branch_1_fun/ppermute | solution.py:18
  296.9 3.5 copy-start.7
  300.4 4.0 copy-start.12
  305.1 27.0 %collective-permute-start.67 = (bf16[512,1152]{1,0:T(8,128)(2,1)S(1)}, bf16[512,1152]{1,0:T(8,128)(2,1)S(1)}, u32[]{:S(2)}, u32[]{:S(2)}) collective-permute-start(bf16[512,1152]{1,0:T(8,128)(2,1)S(1)} %param.40), channel_id=1, source_target_pairs={{0,64},{1,65},{2,66},{3,67},{4,68},{5,69},{6,70},{7,71},{8,72},{9,... | collective-permute-start | bytes 3538952 | tf_op jit(solution)/shard_map/cond/branch_5_fun/ppermute | solution.py:18
  332.1 28.4 %collective-permute-start.68 = (bf16[512,1152]{1,0:T(8,128)(2,1)S(1)}, bf16[512,1152]{1,0:T(8,128)(2,1)}, u32[]{:S(2)}, u32[]{:S(2)}) collective-permute-start(bf16[512,1152]{1,0:T(8,128)(2,1)S(1)} %collective-permute-done.67), channel_id=1, source_target_pairs={{0,128},{1,129},{2,130},{3,131},{4,132},{5,133},{6,134},{7,135},{8... | collective-permute-start | bytes 3538952 | tf_op jit(solution)/shard_map/cond/branch_5_fun/ppermute | solution.py:18
  370.8 25.8 %collective-permute-start.139 = (bf16[512,1152]{1,0:T(8,128)(2,1)S(1)}, bf16[512,1152]{1,0:T(8,128)(2,1)S(1)}, u32[]{:S(2)}, u32[]{:S(2)}) collective-permute-start(bf16[512,1152]{1,0:T(8,128)(2,1)S(1)} %param.82), channel_id=1, source_target_pairs={{0,64},{1,65},{2,66},{3,67},{4,68},{5,69},{6,70},{7,71},{8,72},{9,... | collective-permute-start | bytes 3538952 | tf_op jit(solution)/shard_map/cond/branch_5_fun/ppermute | solution.py:18
  396.6 27.3 %collective-permute-start.140 = (bf16[512,1152]{1,0:T(8,128)(2,1)S(1)}, bf16[512,1152]{1,0:T(8,128)(2,1)}, u32[]{:S(2)}, u32[]{:S(2)}) collective-permute-start(bf16[512,1152]{1,0:T(8,128)(2,1)S(1)} %collective-permute-done.139), channel_id=1, source_target_pairs={{0,128},{1,129},{2,130},{3,131},{4,132},{5,133},{6,134},{7,135},{8... | collective-permute-start | bytes 3538952 | tf_op jit(solution)/shard_map/cond/branch_5_fun/ppermute | solution.py:18
  426.1 24.9 %collective-permute-start.121 = (bf16[512,1152]{1,0:T(8,128)(2,1)S(1)}, bf16[512,1152]{1,0:T(8,128)(2,1)}, u32[]{:S(2)}, u32[]{:S(2)}) collective-permute-start(bf16[512,1152]{1,0:T(8,128)(2,1)S(1)} %param.71), channel_id=1, source_target_pairs={{0,64},{1,65},{2,66},{3,67},{4,68},{5,69},{6,70},{7,71},{8,72},{9,... | collective-permute-start | bytes 3538952 | tf_op jit(solution)/shard_map/cond/branch_1_fun/ppermute | solution.py:18
  453.4 50.2 %collective-permute-start.108 = (bf16[512,1152]{1,0:T(8,128)(2,1)S(1)}, bf16[512,1152]{1,0:T(8,128)(2,1)}, u32[]{:S(2)}, u32[]{:S(2)}) collective-permute-start(bf16[512,1152]{1,0:T(8,128)(2,1)S(1)} %param.63), channel_id=1, source_target_pairs={{0,32},{1,33},{2,34},{3,35},{4,36},{5,37},{6,38},{7,39},{8,40},{9,... | collective-permute-start | bytes 3538952 | tf_op jit(solution)/shard_map/cond/branch_0_fun/ppermute | solution.py:18
  505.8 31.9 %collective-permute-start.98 = (bf16[512,1152]{1,0:T(8,128)(2,1)S(1)}, bf16[512,1152]{1,0:T(8,128)(2,1)S(1)}, u32[]{:S(2)}, u32[]{:S(2)}) collective-permute-start(bf16[512,1152]{1,0:T(8,128)(2,1)S(1)} %param.58), channel_id=1, source_target_pairs={{0,32},{1,33},{2,34},{3,35},{4,36},{5,37},{6,38},{7,39},{8,40},{9,... | collective-permute-start | bytes 3538952 | tf_op jit(solution)/shard_map/cond/branch_2_fun/ppermute | solution.py:18
  537.7 27.1 %collective-permute-start.99 = (bf16[512,1152]{1,0:T(8,128)(2,1)S(1)}, bf16[512,1152]{1,0:T(8,128)(2,1)}, u32[]{:S(2)}, u32[]{:S(2)}) collective-permute-start(bf16[512,1152]{1,0:T(8,128)(2,1)S(1)} %collective-permute-done.98), channel_id=1, source_target_pairs={{0,64},{1,65},{2,66},{3,67},{4,68},{5,69},{6,70},{7,71},{8,72},{9,... | collective-permute-start | bytes 3538952 | tf_op jit(solution)/shard_map/cond/branch_2_fun/ppermute | solution.py:18
  567.3 27.8 %collective-permute-start.88 = (bf16[512,1152]{1,0:T(8,128)(2,1)S(1)}, bf16[512,1152]{1,0:T(8,128)(2,1)}, u32[]{:S(2)}, u32[]{:S(2)}) collective-permute-start(bf16[512,1152]{1,0:T(8,128)(2,1)S(1)} %param.52), channel_id=1, source_target_pairs={{0,128},{1,129},{2,130},{3,131},{4,132},{5,133},{6,134},{7,135},{8... | collective-permute-start | bytes 3538952 | tf_op jit(solution)/shard_map/cond/branch_3_fun/ppermute | solution.py:18
  597.3 29.2 %collective-permute-start.77 = (bf16[512,1152]{1,0:T(8,128)(2,1)S(1)}, bf16[512,1152]{1,0:T(8,128)(2,1)S(1)}, u32[]{:S(2)}, u32[]{:S(2)}) collective-permute-start(bf16[512,1152]{1,0:T(8,128)(2,1)S(1)} %param.46), channel_id=1, source_target_pairs={{0,32},{1,33},{2,34},{3,35},{4,36},{5,37},{6,38},{7,39},{8,40},{9,... | collective-permute-start | bytes 3538952 | tf_op jit(solution)/shard_map/cond/branch_4_fun/ppermute | solution.py:18
  626.5 25.9 %collective-permute-start.78 = (bf16[512,1152]{1,0:T(8,128)(2,1)S(1)}, bf16[512,1152]{1,0:T(8,128)(2,1)}, u32[]{:S(2)}, u32[]{:S(2)}) collective-permute-start(bf16[512,1152]{1,0:T(8,128)(2,1)S(1)} %collective-permute-done.77), channel_id=1, source_target_pairs={{0,128},{1,129},{2,130},{3,131},{4,132},{5,133},{6,134},{7,135},{8... | collective-permute-start | bytes 3538952 | tf_op jit(solution)/shard_map/cond/branch_4_fun/ppermute | solution.py:18
where the time goes:
time: 675 us; the launch traced here: 665 us
  waiting for transfers between devices  537 us (80%)
  matrix products  69.8 us (10%)
  starting transfers between devices  41.1 us (6%)
  between operations  10.5 us (2%)
    ppermute x18, waiting for transfers between devices, from_partner(): return lax.ppermute(value, axis, pairs)  537 us
    ppermute x18, starting transfers between devices, from_partner(): return lax.ppermute(value, axis, pairs)  41.1 us
    dot_general x7, matrix products, pair_tile(): jnp.dot(coefficient, partner, preferred_element_type=jnp.float32)  27.9 us
    dot_general x7, matrix products, rows_by_rows(): lax.dot_general(left, right, (((1,), (1,)), ((), ())), preferred_element_...  24.1 us
    dot_general x7, matrix products, columns_by_columns(): lax.dot_general(left, right, (((0,), (0,)), ((), ())), preferred_element_...  17.8 us
  transfers between devices with their start and end apart: 18, of which 18 were waited for; matrix products, arithmetic and copies ran while one was open for 0% of the time, Pallas kernels for 0%

commit v1 on v0

v1 whole, which is shorter than its diff:
```python
import functools

import jax
import jax.numpy as jnp
from jax import lax
from jax.experimental import pallas as pl
from jax.experimental.pallas import tpu as pltpu
from jax.sharding import PartitionSpec as P

X_SHIFT = 6
Z_BIT = 5
SUB = 256
VMEM_BYTES = 28 << 20


def x_neighbour(index, hop):
    x = index >> X_SHIFT
    return (index & ((1 << X_SHIFT) - 1)) | (((x + hop) & 3) << X_SHIFT)


def to_x(value, hop):
    count = lax.axis_size("dp")
    return lax.ppermute(value, "dp", [(i, x_neighbour(i, hop)) for i in range(count)])


def to_z(value):
    count = lax.axis_size("dp")
    return lax.ppermute(value, "dp", [(i, i ^ (1 << Z_BIT)) for i in range(count)])


def softplus_and_slope(u):
    decay = jnp.exp(-jnp.abs(u))
    ratio = 1.0 / (1.0 + decay)
    slope = jnp.where(u >= 0.0, ratio, decay * ratio)
    return jnp.maximum(u, 0.0) + jnp.log1p(decay), slope


def tiles_kernel(blocks, home, add_to, scalars, flags, images, *rest):
    texts = rest[:blocks]
    rest = rest[blocks:]
    if add_to:
        earlier, rest = rest[0], rest[1:]
    coefs = rest[:blocks]
    grad, losses, scores, total = rest[blocks:]
    rows, width = images.shape
    scale, shift = scalars[0], scalars[1]
    units = [(i, k) for i in range(blocks) for k in range(0, texts[i].shape[0], SUB)]

    def score(unit):
        i, k = unit
        return lax.dot_general(
            texts[i][k : k + SUB, :],
            images[...],
            (((1,), (1,)), ((), ())),
            preferred_element_type=jnp.float32,
        )

    sums = [jnp.zeros((8, rows), jnp.float32) for _ in range(blocks)]
    scores[0] = score(units[0])
    for at, (i, k) in enumerate(units):
        if at + 1 < len(units):
            scores[(at + 1) % 2] = score(units[at + 1])
        u = scale * scores[at % 2] + shift
        if home and i == 0:
            text_row = lax.broadcasted_iota(jnp.int32, (SUB, rows), 0) + k
            diagonal = text_row == lax.broadcasted_iota(jnp.int32, (SUB, rows), 1)
            u = jnp.where(diagonal, -u, u)
        loss, slope = softplus_and_slope(u)
        coef = slope * (scale * flags[i])
        if home and i == 0:
            coef = jnp.where(diagonal, -coef, coef)
        coefs[i][k : k + SUB, :] = coef.astype(jnp.bfloat16)
        sums[i] = sums[i] + jnp.sum(loss.reshape(SUB // 8, 8, rows), axis=0)
        part = lax.dot_general(
            coefs[i][k : k + SUB, :],
            texts[i][k : k + SUB, :],
            (((0,), (0,)), ((), ())),
            preferred_element_type=jnp.float32,
        )
        if at == 0:
            total[...] = earlier[...] + part if add_to else part
        elif at + 1 < len(units):
            total[...] += part
        else:
            grad[...] = (total[...] + part).astype(grad.dtype)
    for i in range(blocks):
        losses[i] = jnp.sum(sums[i])


def tiles(scalars, flags, images, texts, home=False, earlier=None, grad_dtype=jnp.float32):
    blocks = len(texts)
    rows, width = images.shape
    text_rows = sum(t.shape[0] for t in texts)
    vmem = pl.BlockSpec(memory_space=pltpu.VMEM)
    smem = pl.BlockSpec(memory_space=pltpu.SMEM)
    add_to = earlier is not None
    extra = [earlier] if add_to else []
    out = pl.pallas_call(
        functools.partial(tiles_kernel, blocks, home, add_to),
        out_shape=[jax.ShapeDtypeStruct((t.shape[0], rows), jnp.bfloat16) for t in texts]
        + [
            jax.ShapeDtypeStruct((rows, width), grad_dtype),
            jax.ShapeDtypeStruct((blocks,), jnp.float32),
        ],
        in_specs=[smem, smem, vmem] + [vmem] * (blocks + len(extra)),
        out_specs=[vmem] * (blocks + 1) + [smem],
        scratch_shapes=[
            pltpu.VMEM((2, SUB, rows), jnp.float32),
            pltpu.VMEM((rows, width), jnp.float32),
        ],
        compiler_params=pltpu.CompilerParams(vmem_limit_bytes=VMEM_BYTES),
        cost_estimate=pl.CostEstimate(
            flops=4 * rows * text_rows * width,
            bytes_accessed=2 * (rows + text_rows) * width + 2 * rows * text_rows + 4 * rows * width,
            transcendentals=3 * rows * text_rows,
        ),
    )(scalars, flags, images, *texts, *extra)
    return out[:blocks], out[blocks], out[blocks + 1]


def text_kernel(pieces, halves, *refs):
    images = refs[:pieces]
    coefs = refs[pieces : pieces + pieces * halves]
    out = refs[pieces + pieces * halves]
    at = 0
    for h in range(halves):
        size = coefs[h * pieces].shape[0]
        part = None
        for p in range(pieces):
            one = jnp.dot(
                coefs[h * pieces + p][...], images[p][...], preferred_element_type=jnp.float32
            )
            part = one if part is None else part + one
        out[at : at + size, :] = part.astype(out.dtype)
        at += size


def text_partial(images, coefs, dtype):
    pieces, halves = len(images), len(coefs)
    width = images[0].shape[1]
    text_rows = sum(c[0].shape[0] for c in coefs)
    image_rows = sum(i.shape[0] for i in images)
    vmem = pl.BlockSpec(memory_space=pltpu.VMEM)
    flat = [c for run in coefs for c in run]
    return pl.pallas_call(
        functools.partial(text_kernel, pieces, halves),
        out_shape=jax.ShapeDtypeStruct((text_rows, width), dtype),
        in_specs=[vmem] * (pieces + len(flat)),
        out_specs=vmem,
        compiler_params=pltpu.CompilerParams(vmem_limit_bytes=VMEM_BYTES),
        cost_estimate=pl.CostEstimate(
            flops=2 * image_rows * text_rows * width,
            bytes_accessed=2 * image_rows * (text_rows + width) + 4 * text_rows * width,
            transcendentals=0,
        ),
    )(*images, *flat)


def shards(image_embeds, text_embeds, logit_scale, logit_bias, plan):
    pair_rows = image_embeds.shape[0]
    half = pair_rows // 2
    my_index = lax.axis_index("dp")
    round_masks = jnp.right_shift(jnp.bitwise_xor(plan[0], my_index), Z_BIT)
    scalars = jnp.concatenate([logit_scale, logit_bias])

    my_x = my_index >> X_SHIFT
    hops = jnp.array([0, 1, 3, 2, 2], jnp.int32)
    own_masks = ((my_x + hops) & 3 ^ my_x) << 1
    met = lambda masks: jnp.any(round_masks[None, :] == masks[:, None], axis=1)
    own_flags = jnp.where(met(own_masks) | (own_masks == 0), 1.0, 0.0).astype(jnp.float32)
    far_masks = own_masks | 1
    far_flags = jnp.where(met(far_masks), 1.0, 0.0).astype(jnp.float32)

    far_images = [to_z(image_embeds[:half]), to_z(image_embeds[half:])]
    text_below = to_x(text_embeds, 1)
    text_above = to_x(text_embeds, -1)
    text_across = [to_x(text_below[:half], 1), to_x(text_above[half:], -1)]
    near_texts = [text_embeds, text_above, text_below]
    all_texts = near_texts + text_across

    near_coefs, grad_near, loss_near = tiles(
        scalars, own_flags[:3], image_embeds, near_texts, home=True
    )
    far = [
        tiles(scalars, far_flags, images, all_texts, grad_dtype=jnp.bfloat16)
        for images in far_images
    ]
    returned = [to_z(grad) for _, grad, _ in far]
    far_loss = to_z(far[0][2] + far[1][2])
    across_coefs, grad_own, loss_across = tiles(
        scalars, own_flags[3:], image_embeds, text_across, earlier=grad_near
    )

    own_coefs = list(near_coefs) + list(across_coefs)
    images = [image_embeds] + far_images
    runs = [[own_coefs[i], far[0][0][i], far[1][0][i]] for i in range(5)]
    part_across = to_x(text_partial(images, runs[3:], jnp.bfloat16), 2)
    part_above = to_x(text_partial(images, runs[1:2], jnp.bfloat16), 1)
    part_below = to_x(text_partial(images, runs[2:3], jnp.bfloat16), -1)
    text_grad = text_partial(images, runs[:1], jnp.float32)

    text_grad = (
        text_grad
        + part_across.astype(jnp.float32)
        + part_above.astype(jnp.float32)
        + part_below.astype(jnp.float32)
    )
    image_grad = grad_own + jnp.concatenate(returned).astype(jnp.float32)

    sums = jnp.concatenate([loss_near, loss_across, far_loss])
    masks = jnp.concatenate([own_masks, far_masks])
    wanted = jnp.concatenate([jnp.zeros((1,), jnp.int32), round_masks])
    losses = jnp.sum(jnp.where(wanted[:, None] == masks[None, :], sums[None, :], 0.0), axis=1)
    losses = losses / (pair_rows * pair_rows)
    return (image_grad, text_grad, losses[None, :])


def solution(mesh):
    return jax.shard_map(
        shards,
        mesh=mesh,
        in_specs=(P("dp", None), P("dp", None), P(), P(), P("dp", None)),
        out_specs=(P("dp", None), P("dp", None), P("dp", None)),
        check_vma=False,
    )
```

time: 675 us -> 147 us (0.22)
  the two profiles are of different devices: /device:TPU:42 before, /device:TPU:48 now
where the time goes in v1:
time: 147 us
  waiting for transfers between devices  79 us (54%)
  starting transfers between devices  29.7 us (20%)
  Pallas kernels  27.7 us (19%)
  other arithmetic  4.84 us (3%)
  local copies, waits for them, and re-layouts  3.59 us (2%)
  between operations  2.08 us (1%)
    ppermute x7, waiting for transfers between devices, to_x(): lax.ppermute(value, 'dp', [(i, x_neighbour(i, hop)) for i in range(count)])  39.5 us
    ppermute x5, waiting for transfers between devices, to_z(): lax.ppermute(value, 'dp', [(i, i ^ 1 << Z_BIT) for i in range(count)])  39.5 us
    pallas_call x4, Pallas kernels, tiles(): pl.pallas_call(functools.partial(tiles_kernel, blocks, home, add_to), out...  21.5 us
    ppermute x5, starting transfers between devices, to_z(): lax.ppermute(value, 'dp', [(i, i ^ 1 << Z_BIT) for i in range(count)])  18.1 us
    ppermute x7, starting transfers between devices, to_x(): lax.ppermute(value, 'dp', [(i, x_neighbour(i, hop)) for i in range(count)])  11.6 us
    pallas_call x4, Pallas kernels, text_partial(): pl.pallas_call(functools.partial(text_kernel, pieces, halves), out_shape=...  6.2 us
  transfers between devices with their start and end apart: 12, of which 6 were waited for; matrix products, arithmetic and copies ran while one was open for 4% of the time, Pallas kernels for 19%

profile of v1, /device:TPU:48, one launch (start us, length us, event | category | flops | bytes accessed | tf_op | source)
XLA Modules:
  0.0 146.9 jit_solution(17118725242192246458)
XLA Ops:
  0.7 2.8 %collective-permute-start.2 = (bf16[512,1152]{1,0:T(8,128)(2,1)}, bf16[512,1152]{1,0:T(8,128)(2,1)S(1)}, u32[]{:S(2)}, u32[]{:S(2)}) collective-permute-start(bf16[512,1152]{1,0:T(8,128)(2,1)} %rest_0_.5), channel_id=1, source_target_pairs={{0,192},{1,193},{2,194},{3,195},{4,196},{5,197},{6,198},{7,199},{8... | collective-permute-start | bytes 3538952 | tf_op jit(solution)/shard_map/ppermute | solution.py:23
  3.5 2.3 %fusion = (bf16[256,1152]{1,0:T(8,128)(2,1)}, bf16[256,1152]{1,0:T(8,128)(2,1)}) fusion(bf16[512,1152]{1,0:T(8,128)(2,1)} %refs_0_.7), kind=kLoop, calls=%fused_computation.15 | loop fusion | bytes 2359296 | tf_op jit(solution)/shard_map/slice | solution.py:174
  5.8 6.3 %collective-permute-start.4 = (bf16[256,1152]{1,0:T(8,128)(2,1)}, bf16[256,1152]{1,0:T(8,128)(2,1)S(1)}, u32[]{:S(2)}, u32[]{:S(2)}) collective-permute-start(bf16[256,1152]{1,0:T(8,128)(2,1)} %get-tuple-element.53), channel_id=1, source_target_pairs={{0,32},{1,33},{2,34},{3,35},{4,36},{5,37},{6,38},{7,39},{8,40},{9,... | collective-permute-start | bytes 1769480 | tf_op jit(solution)/shard_map/ppermute | solution.py:28
  12.2 0.2 compare_reduce_fusion
  12.4 16.6 %collective-permute-done.2.rest_1_ = bf16[512,1152]{1,0:T(8,128)(2,1)S(1)} collective-permute-done((bf16[512,1152]{1,0:T(8,128)(2,1)}, bf16[512,1152]{1,0:T(8,128)(2,1)S(1)}, u32[]{:S(2)}, u32[]{:S(2)}) %collective-permute-start.2) | collective-permute-done | bytes 1179680 | tf_op jit(solution)/shard_map/ppermute | solution.py:23
  29.1 3.7 %collective-permute-start.3 = (bf16[256,1152]{1,0:T(8,128)(2,1)S(1)}, bf16[256,1152]{1,0:T(8,128)(2,1)S(1)}, u32[]{:S(2)}, u32[]{:S(2)}) collective-permute-start(bf16[256,1152]{1,0:T(8,128)(2,1)S(1)} %slice.25), channel_id=1, source_target_pairs={{0,192},{1,193},{2,194},{3,195},{4,196},{5,197},{6,198},{7,199},{8... | collective-permute-start | bytes 1769480 | tf_op jit(solution)/shard_map/ppermute | solution.py:23
  32.8 1.1 slice.24
  33.9 0.3 collective-permute-start.1
  35.7 7.1 %shard_map.85 = (bf16[512,512]{1,0:T(8,128)(2,1)S(1)}, bf16[512,512]{1,0:T(8,128)(2,1)S(1)}, bf16[512,512]{1,0:T(8,128)(2,1)S(1)}, f32[512,1152]{1,0:T(8,128)S(1)}, f32[3]{0:T(128)S(1)}) custom-call(f32[2]{0:T(128)S(1)} %pad_maximum_fusion.scalars, f32[3]{0:T(128)S(1)} %bitcast.5, bf16[512,1152]{1,0:T(8,128)(2,1)S(1)} %copy-done, ...), custom_call_target="tpu_custom_call" | custom-call | flops 3623878656 | bytes 8650752 | tf_op jit(solution)/shard_map/pallas_call | solution.py:98
  42.8 20.8 %collective-permute-done.6.images.refs_2_ = bf16[256,1152]{1,0:T(8,128)(2,1)S(1)} collective-permute-done((bf16[256,1152]{1,0:T(8,128)(2,1)}, bf16[256,1152]{1,0:T(8,128)(2,1)S(1)}, u32[]{:S(2)}, u32[]{:S(2)}) %collective-permute-start.6) | collective-permute-done | bytes 589856 | tf_op jit(solution)/shard_map/ppermute | solution.py:28
  63.6 5.8 %shard_map.88 = (bf16[512,256]{1,0:T(8,128)(2,1)S(1)}, bf16[512,256]{1,0:T(8,128)(2,1)S(1)}, bf16[512,256]{1,0:T(8,128)(2,1)S(1)}, bf16[256,256]{1,0:T(8,128)(2,...) custom-call(f32[2]{0:T(128)S(1)} %pad_maximum_fusion.scalars, ...), custom_call_target="tpu_custom_call" | custom-call | flops 2415919104 | bytes 7536640 | tf_op jit(solution)/shard_map/pallas_call | solution.py:98
  69.4 5.7 %collective-permute-start.7 = (bf16[256,1152]{1,0:T(8,128)(2,1)S(1)}, bf16[256,1152]{1,0:T(8,128)(2,1)S(1)}, u32[]{:S(2)}, u32[]{:S(2)}) collective-permute-start(bf16[256,1152]{1,0:T(8,128)(2,1)S(1)} %get-tuple-element.29), channel_id=1, source_target_pairs={{0,32},{1,33},{2,34},{3,35},{4,36},{5,37},{6,38},{7,39},{8,40},{9,... | collective-permute-start | bytes 1769480 | tf_op jit(solution)/shard_map/ppermute | solution.py:28
  75.2 5.8 %shard_map.87 = (bf16[512,256]{1,0:T(8,128)(2,1)S(1)}, bf16[512,256]{1,0:T(8,128)(2,1)S(1)}, bf16[512,256]{1,0:T(8,128)(2,1)S(1)}, bf16[256,256]{1,0:T(8,128)(2,...) custom-call(f32[2]{0:T(128)S(1)} %pad_maximum_fusion.scalars, ...), custom_call_target="tpu_custom_call" | custom-call | flops 2415919104 | bytes 7536640 | tf_op jit(solution)/shard_map/pallas_call | solution.py:98
  81.0 0.6 collective-permute-start.11
  81.6 5.4 %collective-permute-start.5 = (bf16[256,1152]{1,0:T(8,128)(2,1)S(1)}, bf16[256,1152]{1,0:T(8,128)(2,1)S(1)}, u32[]{:S(2)}, u32[]{:S(2)}) collective-permute-start(bf16[256,1152]{1,0:T(8,128)(2,1)S(1)} %get-tuple-element.28), channel_id=1, source_target_pairs={{0,32},{1,33},{2,34},{3,35},{4,36},{5,37},{6,38},{7,39},{8,40},{9,... | collective-permute-start | bytes 1769480 | tf_op jit(solution)/shard_map/ppermute | solution.py:28
  87.0 1.6 %shard_map.92 = bf16[512,1152]{1,0:T(8,128)(2,1)S(1)} custom-call(bf16[512,1152]{1,0:T(8,128)(2,1)S(1)} %copy-done, bf16[256,1152]{1,0:T(8,128)(2,1)S(1)} %collective-permute-done.4.images.refs_1_, bf16[256,1152]{1,0:T(8,128)(2,1)S(1)} %collective-permute-done.6.images.refs_2_, bf16[512,512]{1,0:T(8,128)(2,1)S(1)} %get-tuple-element.42.refs_3_, ...), custom_call_target="tpu_custom_call" | custom-call | flops 1207959552 | bytes 5767168 | tf_op jit(solution)/shard_map/pallas_call | solution.py:145
  88.6 3.0 %collective-permute-start.10 = (bf16[512,1152]{1,0:T(8,128)(2,1)S(1)}, bf16[512,1152]{1,0:T(8,128)(2,1)S(1)}, u32[]{:S(2)}, u32[]{:S(2)}) collective-permute-start(bf16[512,1152]{1,0:T(8,128)(2,1)S(1)} %shard_map.92), channel_id=1, source_target_pairs={{0,192},{1,193},{2,194},{3,195},{4,196},{5,197},{6,198},{7,199},{8... | collective-permute-start | bytes 3538952 | tf_op jit(solution)/shard_map/ppermute | solution.py:23
  91.6 1.6 %shard_map.91 = bf16[512,1152]{1,0:T(8,128)(2,1)S(1)} custom-call(bf16[512,1152]{1,0:T(8,128)(2,1)S(1)} %copy-done, bf16[256,1152]{1,0:T(8,128)(2,1)S(1)} %collective-permute-done.4.images.refs_1_, bf16[256,1152]{1,0:T(8,128)(2,1)S(1)} %collective-permute-done.6.images.refs_2_, bf16[512,512]{1,0:T(8,128)(2,1)S(1)} %get-tuple-element.39.refs_3_, ...), custom_call_target="tpu_custom_call" | custom-call | flops 1207959552 | bytes 5767168 | tf_op jit(solution)/shard_map/pallas_call | solution.py:145
  93.2 0.1 collective-permute-start.9
  93.3 2.8 %shard_map.86 = (bf16[256,512]{1,0:T(8,128)(2,1)S(1)}, bf16[256,512]{1,0:T(8,128)(2,1)S(1)}, f32[512,1152]{1,0:T(8,128)S(1)}, f32[2]{0:T(128)S(1)}) custom-call(f32[2]{0:T(128)S(1)} %pad_maximum_fusion.scalars, f32[2]{0:T(128)S(1)} %slice.18.flags, bf16[512,1152]{1,0:T(8,128)(2,1)S(1)} %copy-done, ...), custom_call_target="tpu_custom_call" | custom-call | flops 1207959552 | bytes 5242880 | tf_op jit(solution)/shard_map/pallas_call | solution.py:98
  96.1 1.5 %shard_map.90 = bf16[512,1152]{1,0:T(8,128)(2,1)S(1)} custom-call(bf16[512,1152]{1,0:T(8,128)(2,1)S(1)} %copy-done, bf16[256,1152]{1,0:T(8,128)(2,1)S(1)} %collective-permute-done.4.images.refs_1_, bf16[256,1152]{1,0:T(8,128)(2,1)S(1)} %collective-permute-done.6.images.refs_2_, bf16[256,512]{1,0:T(8,128)(2,1)S(1)} %get-tuple-element.33.refs_3_, ...), custom_call_target="tpu_custom_call" | custom-call | flops 1207959552 | bytes 5767168 | tf_op jit(solution)/shard_map/pallas_call | solution.py:145
  97.7 10.2 %collective-permute-done.11 = f32[5]{0:T(128)S(1)} collective-permute-done((f32[5]{0:T(128)S(1)}, f32[5]{0:T(128)S(1)}, u32[]{:S(2)}, u32[]{:S(2)}) %collective-permute-start.11) | collective-permute-done | bytes 52 | tf_op jit(solution)/shard_map/ppermute | solution.py:28
  107.9 1.7 %collective-permute-start.8 = (bf16[512,1152]{1,0:T(8,128)(2,1)S(1)}, bf16[512,1152]{1,0:T(8,128)(2,1)S(1)}, u32[]{:S(2)}, u32[]{:S(2)}) collective-permute-start(bf16[512,1152]{1,0:T(8,128)(2,1)S(1)} %shard_map.90), channel_id=1, source_target_pairs={{0,128},{1,129},{2,130},{3,131},{4,132},{5,133},{6,134},{7,135},{8... | collective-permute-start | bytes 3538952 | tf_op jit(solution)/shard_map/ppermute | solution.py:23
  109.6 1.5 %shard_map.89 = f32[512,1152]{1,0:T(8,128)S(1)} custom-call(bf16[512,1152]{1,0:T(8,128)(2,1)S(1)} %copy-done, bf16[256,1152]{1,0:T(8,128)(2,1)S(1)} %collective-permute-done.4.images.refs_1_, bf16[256,1152]{1,0:T(8,128)(2,1)S(1)} %collective-permute-done.6.images.refs_2_, bf16[512,512]{1,0:T(8,128)(2,1)S(1)} %get-tuple-element.30.refs_3_, ...), custom_call_target="tpu_custom_call" | custom-call | flops 1207959552 | bytes 5767168 | tf_op jit(solution)/shard_map/pallas_call | solution.py:145
  111.2 0.1 pad_maximum_fusion.1
  111.3 0.2 select_reduce_fusion
  111.5 0.5 multiply_bitcast_fusion
  112.0 8.4 %collective-permute-done.5 = bf16[256,1152]{1,0:T(8,128)(2,1)S(1)} collective-permute-done((bf16[256,1152]{1,0:T(8,128)(2,1)S(1)}, bf16[256,1152]{1,0:T(8,128)(2,1)S(1)}, u32[]{:S(2)}, u32[]{:S(2)}) %collective-permute-start.5) | collective-permute-done | bytes 589856 | tf_op jit(solution)/shard_map/ppermute | solution.py:28
  120.4 1.6 %convert_add_fusion.1 = f32[512,1152]{1,0:T(8,128)} fusion(f32[512,1152]{1,0:T(8,128)S(1)} %get-tuple-element.27, bf16[256,1152]{1,0:T(8,128)(2,1)S(1)} %collective-permute-done.7, bf16[256,1152]{1,0:T(8,128)(2,1)S(1)} %collective-permute-done.5), kind=kLoop, calls=%fused_computation.1 | loop fusion | flops 2949120 | bytes 5898240 | tf_op jit(solution)/shard_map/add | solution.py:208
  122.0 17.9 %collective-permute-done.10 = bf16[512,1152]{1,0:T(8,128)(2,1)S(1)} collective-permute-done((bf16[512,1152]{1,0:T(8,128)(2,1)S(1)}, bf16[512,1152]{1,0:T(8,128)(2,1)S(1)}, u32[]{:S(2)}, u32[]{:S(2)}) %collective-permute-start.10) | collective-permute-done | bytes 1179680 | tf_op jit(solution)/shard_map/ppermute | solution.py:23
  139.9 5.0 %collective-permute-done.9 = bf16[512,1152]{1,0:T(8,128)(2,1)S(1)} collective-permute-done((bf16[512,1152]{1,0:T(8,128)(2,1)S(1)}, bf16[512,1152]{1,0:T(8,128)(2,1)S(1)}, u32[]{:S(2)}, u32[]{:S(2)}) %collective-permute-start.9) | collective-permute-done | bytes 1179680 | tf_op jit(solution)/shard_map/ppermute | solution.py:23
  144.9 2.0 %convert_add_fusion = f32[512,1152]{1,0:T(8,128)} fusion(bf16[512,1152]{1,0:T(8,128)(2,1)S(1)} %collective-permute-done.10, bf16[512,1152]{1,0:T(8,128)(2,1)S(1)} %collective-permute-done.9, f32[512,1152]{1,0:T(8,128)S(1)} %shard_map.89, bf16[512,1152]{1,0:T(8,128)(2,1)S(1)} %collective-permute-done.8), kind=kLoop, calls=%fused_computation | loop fusion | flops 3538944 | bytes 8257536 | tf_op jit(solution)/shard_map/add | solution.py:203
  (26 shorter events, 0.4 us)
Async XLA Ops:
  0.6 11.5 %copy-start.2 = (s32[5]{0:T(128)S(1)}, s32[5]{0:T(128)}, u32[]{:S(2)}) copy-start(s32[5]{0:T(128)} %constant.27.clone) | copy-start | bytes 64
  0.6 35.1 %copy-start = (bf16[512,1152]{1,0:T(8,128)(2,1)S(1)}, bf16[512,1152]{1,0:T(8,128)(2,1)}, u32[]{:S(2)}) copy-start(bf16[512,1152]{1,0:T(8,128)(2,1)} %refs_0_.7) | copy-start | bytes 3538948
  0.7 11.5 %copy-start.3 = (s32[1,6]{1,0:T(1,128)S(1)}, s32[1,6]{1,0:T(1,128)}, u32[]{:S(2)}) copy-start(s32[1,6]{1,0:T(1,128)} %param.10) | copy-start | bytes 76
  0.7 28.4 %collective-permute-start.2 = (bf16[512,1152]{1,0:T(8,128)(2,1)}, bf16[512,1152]{1,0:T(8,128)(2,1)S(1)}, u32[]{:S(2)}, u32[]{:S(2)}) collective-permute-start(bf16[512,1152]{1,0:T(8,128)(2,1)} %rest_0_.5), channel_id=1, source_target_pairs={{0,192},{1,193},{2,194},{3,195},{4,196},{5,197},{6,198},{7,199},{8... | collective-permute-start | bytes 3538952 | tf_op jit(solution)/shard_map/ppermute | solution.py:23
  3.5 29.3 %collective-permute-start = (bf16[512,1152]{1,0:T(8,128)(2,1)}, bf16[512,1152]{1,0:T(8,128)(2,1)}, u32[]{:S(2)}, u32[]{:S(2)}) collective-permute-start(bf16[512,1152]{1,0:T(8,128)(2,1)} %rest_0_.5), channel_id=1, source_target_pairs={{0,64},{1,65},{2,66},{3,67},{4,68},{5,69},{6,70},{7,71},{8,72},{9,... | collective-permute-start | bytes 3538952 | tf_op jit(solution)/shard_map/ppermute | solution.py:23
  5.8 69.3 %collective-permute-start.4 = (bf16[256,1152]{1,0:T(8,128)(2,1)}, bf16[256,1152]{1,0:T(8,128)(2,1)S(1)}, u32[]{:S(2)}, u32[]{:S(2)}) collective-permute-start(bf16[256,1152]{1,0:T(8,128)(2,1)} %get-tuple-element.53), channel_id=1, source_target_pairs={{0,32},{1,33},{2,34},{3,35},{4,36},{5,37},{6,38},{7,39},{8,40},{9,... | collective-permute-start | bytes 1769480 | tf_op jit(solution)/shard_map/ppermute | solution.py:28
  12.1 51.5 %collective-permute-start.6 = (bf16[256,1152]{1,0:T(8,128)(2,1)}, bf16[256,1152]{1,0:T(8,128)(2,1)S(1)}, u32[]{:S(2)}, u32[]{:S(2)}) collective-permute-start(bf16[256,1152]{1,0:T(8,128)(2,1)} %get-tuple-element.54), channel_id=1, source_target_pairs={{0,32},{1,33},{2,34},{3,35},{4,36},{5,37},{6,38},{7,39},{8,40},{9,... | collective-permute-start | bytes 1769480 | tf_op jit(solution)/shard_map/ppermute | solution.py:28
  12.2 23.6 %copy-start.1 = (bf16[512,1152]{1,0:T(8,128)(2,1)S(1)}, bf16[512,1152]{1,0:T(8,128)(2,1)}, u32[]{:S(2)}) copy-start(bf16[512,1152]{1,0:T(8,128)(2,1)} %rest_0_.5) | copy-start | bytes 3538948
  29.1 34.5 %collective-permute-start.3 = (bf16[256,1152]{1,0:T(8,128)(2,1)S(1)}, bf16[256,1152]{1,0:T(8,128)(2,1)S(1)}, u32[]{:S(2)}, u32[]{:S(2)}) collective-permute-start(bf16[256,1152]{1,0:T(8,128)(2,1)S(1)} %slice.25), channel_id=1, source_target_pairs={{0,192},{1,193},{2,194},{3,195},{4,196},{5,197},{6,198},{7,199},{8... | collective-permute-start | bytes 1769480 | tf_op jit(solution)/shard_map/ppermute | solution.py:23
  33.9 29.7 %collective-permute-start.1 = (bf16[256,1152]{1,0:T(8,128)(2,1)S(1)}, bf16[256,1152]{1,0:T(8,128)(2,1)S(1)}, u32[]{:S(2)}, u32[]{:S(2)}) collective-permute-start(bf16[256,1152]{1,0:T(8,128)(2,1)S(1)} %slice.24), channel_id=1, source_target_pairs={{0,64},{1,65},{2,66},{3,67},{4,68},{5,69},{6,70},{7,71},{8,72},{9,... | collective-permute-start | bytes 1769480 | tf_op jit(solution)/shard_map/ppermute | solution.py:23
  69.4 42.5 %collective-permute-start.7 = (bf16[256,1152]{1,0:T(8,128)(2,1)S(1)}, bf16[256,1152]{1,0:T(8,128)(2,1)S(1)}, u32[]{:S(2)}, u32[]{:S(2)}) collective-permute-start(bf16[256,1152]{1,0:T(8,128)(2,1)S(1)} %get-tuple-element.29), channel_id=1, source_target_pairs={{0,32},{1,33},{2,34},{3,35},{4,36},{5,37},{6,38},{7,39},{8,40},{9,... | collective-permute-start | bytes 1769480 | tf_op jit(solution)/shard_map/ppermute | solution.py:28
  81.0 26.9 %collective-permute-start.11 = (f32[5]{0:T(128)S(1)}, f32[5]{0:T(128)S(1)}, u32[]{:S(2)}, u32[]{:S(2)}) collective-permute-start(f32[5]{0:T(128)S(1)} %add.27), channel_id=1, source_target_pairs={{0,32},{1,33},{2,34},{3,35},{4,36},{5,37},{6,38},{7,39},{8,40},{9,... | collective-permute-start | bytes 68 | tf_op jit(solution)/shard_map/ppermute | solution.py:28
  81.6 38.8 %collective-permute-start.5 = (bf16[256,1152]{1,0:T(8,128)(2,1)S(1)}, bf16[256,1152]{1,0:T(8,128)(2,1)S(1)}, u32[]{:S(2)}, u32[]{:S(2)}) collective-permute-start(bf16[256,1152]{1,0:T(8,128)(2,1)S(1)} %get-tuple-element.28), channel_id=1, source_target_pairs={{0,32},{1,33},{2,34},{3,35},{4,36},{5,37},{6,38},{7,39},{8,40},{9,... | collective-permute-start | bytes 1769480 | tf_op jit(solution)/shard_map/ppermute | solution.py:28
  88.6 51.3 %collective-permute-start.10 = (bf16[512,1152]{1,0:T(8,128)(2,1)S(1)}, bf16[512,1152]{1,0:T(8,128)(2,1)S(1)}, u32[]{:S(2)}, u32[]{:S(2)}) collective-permute-start(bf16[512,1152]{1,0:T(8,128)(2,1)S(1)} %shard_map.92), channel_id=1, source_target_pairs={{0,192},{1,193},{2,194},{3,195},{4,196},{5,197},{6,198},{7,199},{8... | collective-permute-start | bytes 3538952 | tf_op jit(solution)/shard_map/ppermute | solution.py:23
  93.2 51.7 %collective-permute-start.9 = (bf16[512,1152]{1,0:T(8,128)(2,1)S(1)}, bf16[512,1152]{1,0:T(8,128)(2,1)S(1)}, u32[]{:S(2)}, u32[]{:S(2)}) collective-permute-start(bf16[512,1152]{1,0:T(8,128)(2,1)S(1)} %shard_map.91), channel_id=1, source_target_pairs={{0,64},{1,65},{2,66},{3,67},{4,68},{5,69},{6,70},{7,71},{8,72},{9,... | collective-permute-start | bytes 3538952 | tf_op jit(solution)/shard_map/ppermute | solution.py:23
  107.9 37.0 %collective-permute-start.8 = (bf16[512,1152]{1,0:T(8,128)(2,1)S(1)}, bf16[512,1152]{1,0:T(8,128)(2,1)S(1)}, u32[]{:S(2)}, u32[]{:S(2)}) collective-permute-start(bf16[512,1152]{1,0:T(8,128)(2,1)S(1)} %shard_map.90), channel_id=1, source_target_pairs={{0,128},{1,129},{2,130},{3,131},{4,132},{5,133},{6,134},{7,135},{8... | collective-permute-start | bytes 3538952 | tf_op jit(solution)/shard_map/ppermute | solution.py:23

commit v2 on v1

v2 whole, which is shorter than its diff:
```python
import functools

import jax
import jax.numpy as jnp
from jax import lax
from jax.experimental import pallas as pl
from jax.experimental.pallas import tpu as pltpu
from jax.sharding import PartitionSpec as P

X_SHIFT = 6
Z_BIT = 5
SUB = 256
FIRST = 256
VMEM_BYTES = 16 << 20
SMALL = pl.CostEstimate(flops=1024, bytes_accessed=1024, transcendentals=0)
MIDDLE = pl.CostEstimate(flops=1 << 31, bytes_accessed=1 << 20, transcendentals=0)
LARGE = pl.CostEstimate(flops=1 << 34, bytes_accessed=1 << 20, transcendentals=0)

ANY = pl.BlockSpec(memory_space=pl.ANY)
VMEM = pl.BlockSpec(memory_space=pltpu.VMEM)
SMEM = pl.BlockSpec(memory_space=pltpu.SMEM)


def x_neighbour(index, hop):
    x = index >> X_SHIFT
    return (index & ((1 << X_SHIFT) - 1)) | (((x + hop) & 3) << X_SHIFT)


def to_x(value, hop):
    count = lax.axis_size("dp")
    return lax.ppermute(value, "dp", [(i, x_neighbour(i, hop)) for i in range(count)])


def to_z(value):
    count = lax.axis_size("dp")
    return lax.ppermute(value, "dp", [(i, i ^ (1 << Z_BIT)) for i in range(count)])


def stage_kernel(starts, *refs):
    count = len(starts)
    sources, targets, sems = refs[:count], refs[-1 - count : -1], refs[-1]
    copies = [
        pltpu.make_async_copy(
            sources[i].at[pl.ds(starts[i], targets[i].shape[0]), :], targets[i], sems.at[i]
        )
        for i in range(count)
    ]
    for copy in copies:
        copy.start()
    for copy in copies:
        copy.wait()


def staged(parts):
    count = len(parts)
    return pl.pallas_call(
        functools.partial(stage_kernel, [first for _, first, _ in parts]),
        out_shape=[
            jax.ShapeDtypeStruct((rows, value.shape[1]), value.dtype) for value, _, rows in parts
        ],
        in_specs=[ANY] * count,
        out_specs=[VMEM] * count,
        scratch_shapes=[pltpu.SemaphoreType.DMA((count,))],
        compiler_params=pltpu.CompilerParams(vmem_limit_bytes=60 << 20),
        cost_estimate=SMALL,
    )(*[value for value, _, _ in parts])


def softplus_and_slope(u):
    decay = jnp.exp(-jnp.abs(u))
    ratio = 1.0 / (1.0 + decay)
    slope = jnp.where(u >= 0.0, ratio, decay * ratio)
    return jnp.maximum(u, 0.0) + jnp.log1p(decay), slope


def rows_by_rows(left, right):
    return lax.dot_general(
        left, right, (((1,), (1,)), ((), ())), preferred_element_type=jnp.float32
    )


def columns_by_columns(left, right):
    return lax.dot_general(
        left, right, (((0,), (0,)), ((), ())), preferred_element_type=jnp.float32
    )


def units_of(texts):
    return [(i, k) for i in range(len(texts)) for k in range(0, texts[i].shape[0], SUB)]


def tiles_kernel(blocks, home, add_to, with_grad, scalars, flags, after, images, *rest):
    texts = rest[:blocks]
    rest = rest[blocks:]
    if add_to:
        earlier, rest = rest[0], rest[1:]
    coefs, rest = rest[:blocks], rest[blocks:]
    if with_grad:
        grad, losses, scores, total = rest
    else:
        losses, scores = rest
    rows = images.shape[0]
    scale, shift = scalars[0], scalars[1]
    units = units_of(texts)

    def score(unit):
        i, k = unit
        return rows_by_rows(texts[i][k : k + SUB, :], images[...])

    sums = [jnp.zeros((8, rows), jnp.float32) for _ in range(blocks)]
    scores[0] = score(units[0])
    for at, (i, k) in enumerate(units):
        if at + 1 < len(units):
            scores[(at + 1) % 2] = score(units[at + 1])
        u = scale * scores[at % 2] + shift
        if home and i == 0:
            text_row = lax.broadcasted_iota(jnp.int32, (SUB, rows), 0) + k
            diagonal = text_row == lax.broadcasted_iota(jnp.int32, (SUB, rows), 1)
            u = jnp.where(diagonal, -u, u)
        loss, slope = softplus_and_slope(u)
        coef = slope * (scale * flags[i])
        if home and i == 0:
            coef = jnp.where(diagonal, -coef, coef)
        coefs[i][k : k + SUB, :] = coef.astype(jnp.bfloat16)
        sums[i] = sums[i] + jnp.sum(loss.reshape(SUB // 8, 8, rows), axis=0)
        if with_grad:
            part = columns_by_columns(coefs[i][k : k + SUB, :], texts[i][k : k + SUB, :])
            if at == 0:
                total[...] = earlier[...] + part if add_to else part
            elif at + 1 < len(units):
                total[...] += part
            else:
                grad[...] = (total[...] + part).astype(grad.dtype)
    for i in range(blocks):
        losses[i] = jnp.sum(sums[i])


def tiles(
    scalars, flags, after, images, texts, home=False, earlier=None, grad_dtype=jnp.float32
):
    blocks = len(texts)
    rows, width = images.shape
    extra = [] if earlier is None else [earlier]
    with_grad = grad_dtype is not None
    grad = [jax.ShapeDtypeStruct((rows, width), grad_dtype)] if with_grad else []
    total = [pltpu.VMEM((rows, width), jnp.float32)] if with_grad else []
    out = pl.pallas_call(
        functools.partial(tiles_kernel, blocks, home, len(extra) > 0, with_grad),
        out_shape=[jax.ShapeDtypeStruct((t.shape[0], rows), jnp.bfloat16) for t in texts]
        + grad
        + [jax.ShapeDtypeStruct((blocks,), jnp.float32)],
        in_specs=[SMEM, SMEM, SMEM, VMEM] + [VMEM] * (blocks + len(extra)),
        out_specs=[VMEM] * (blocks + len(grad)) + [SMEM],
        scratch_shapes=[pltpu.VMEM((2, SUB, rows), jnp.float32)] + total,
        compiler_params=pltpu.CompilerParams(vmem_limit_bytes=VMEM_BYTES),
        cost_estimate=SMALL,
    )(scalars, flags, after, images, *texts, *extra)
    return list(out[:blocks]), out[blocks], out[-1]


def image_grad_kernel(blocks, *refs):
    texts, coefs = refs[:blocks], refs[blocks : 2 * blocks]
    first_losses, second_losses = refs[2 * blocks : 2 * blocks + 2]
    grad, losses, total = refs[-3:]
    for i in range(blocks):
        losses[i] = first_losses[i] + second_losses[i]
    for i in range(blocks):
        part = columns_by_columns(coefs[i][...], texts[i][...])
        if i == 0:
            total[...] = part
        elif i + 1 < blocks:
            total[...] += part
        else:
            grad[...] = (total[...] + part).astype(grad.dtype)


def image_partial(texts, coefs, losses, after):
    blocks = len(texts)
    rows, width = coefs[0].shape[1], texts[0].shape[1]
    return pl.pallas_call(
        functools.partial(image_grad_kernel, blocks),
        out_shape=[
            jax.ShapeDtypeStruct((rows, width), jnp.bfloat16),
            jax.ShapeDtypeStruct((blocks,), jnp.float32),
        ],
        in_specs=[VMEM] * (2 * blocks) + [SMEM] * 2 + [ANY] * len(after),
        out_specs=[VMEM, SMEM],
        scratch_shapes=[pltpu.VMEM((rows, width), jnp.float32)],
        compiler_params=pltpu.CompilerParams(vmem_limit_bytes=VMEM_BYTES),
        cost_estimate=SMALL,
    )(*texts, *coefs, *losses, *after)


def text_kernel(pieces, runs, added, passed, *refs):
    images = refs[:pieces]
    coefs = refs[pieces : pieces + pieces * len(runs)]
    earlier = refs[pieces + pieces * len(runs) :][:added]
    outs = refs[len(refs) - len(runs) - passed :]
    if passed:
        given = refs[pieces + pieces * len(runs) + added]
        for i in range(given.shape[0]):
            outs[-1][i] = given[i]
    for r, (first, rows) in enumerate(runs):
        part = None
        for p in range(pieces):
            one = jnp.dot(
                coefs[r * pieces + p][first : first + rows, :],
                images[p][...],
                preferred_element_type=jnp.float32,
            )
            part = one if part is None else part + one
        if added:
            part = part + earlier[r][...].astype(jnp.float32)
        outs[r][...] = part.astype(outs[r].dtype)


def text_partials(images, runs, dtype, earlier=(), passed=(), after=(), cost=SMALL):
    width = images[0].shape[1]
    flat = [c for coefs, _, _ in runs for c in coefs]
    return pl.pallas_call(
        functools.partial(
            text_kernel, len(images), [(first, rows) for _, first, rows in runs], len(earlier), len(passed)
        ),
        out_shape=[jax.ShapeDtypeStruct((rows, width), dtype) for _, _, rows in runs]
        + [jax.ShapeDtypeStruct(p.shape, p.dtype) for p in passed],
        in_specs=[VMEM] * (len(images) + len(flat) + len(earlier))
        + [SMEM] * len(passed)
        + [ANY] * len(after),
        out_specs=[VMEM] * len(runs) + [SMEM] * len(passed),
        compiler_params=pltpu.CompilerParams(vmem_limit_bytes=VMEM_BYTES),
        cost_estimate=cost,
    )(*images, *flat, *earlier, *passed, *after)


def add_kernel(base, block, *refs):
    out, token = refs[-2:]
    out[...] = base[...] + block[...].astype(jnp.float32)
    token[0] = 0.0


def add_rows(base, block, first, into=None, cost=SMALL):
    rows, width = block.shape
    step_rows = rows // 2
    offset = first // step_rows
    rest = [] if into is None else [into]
    return pl.pallas_call(
        add_kernel,
        grid=(2,),
        out_shape=[
            jax.ShapeDtypeStruct(base.shape, jnp.float32),
            jax.ShapeDtypeStruct((1,), jnp.float32),
        ],
        in_specs=[
            pl.BlockSpec((step_rows, width), lambda i: (i + offset, 0)),
            pl.BlockSpec((step_rows, width), lambda i: (i, 0)),
        ]
        + [ANY] * len(rest),
        out_specs=[pl.BlockSpec((step_rows, width), lambda i: (i + offset, 0)), SMEM],
        input_output_aliases={2: 0} if rest else {},
        compiler_params=pltpu.CompilerParams(vmem_limit_bytes=VMEM_BYTES),
        cost_estimate=cost,
    )(base, block, *rest)


def join_kernel(low, high, low_more, high_more, out):
    step = pl.program_id(0)

    @pl.when(step == 0)
    def _():
        out[...] = low[...] + low_more[...].astype(jnp.float32)

    @pl.when(step == 1)
    def _():
        out[...] = high[...] + high_more[...].astype(jnp.float32)


def joined(low, high, low_more, high_more):
    rows, width = low.shape
    return pl.pallas_call(
        join_kernel,
        grid=(2,),
        out_shape=jax.ShapeDtypeStruct((2 * rows, width), jnp.float32),
        in_specs=[VMEM] * 4,
        out_specs=pl.BlockSpec((rows, width), lambda i: (i, 0)),
        compiler_params=pltpu.CompilerParams(vmem_limit_bytes=VMEM_BYTES),
        cost_estimate=SMALL,
    )(low, high, low_more, high_more)


def shards(image_embeds, text_embeds, logit_scale, logit_bias, plan):
    pair_rows = image_embeds.shape[0]
    half = pair_rows // 2
    my_index = lax.axis_index("dp")
    round_masks = jnp.right_shift(jnp.bitwise_xor(plan[0], my_index), Z_BIT)
    scalars = jnp.concatenate([logit_scale, logit_bias])

    my_x = my_index >> X_SHIFT
    hops = jnp.array([0, 1, 3, 2, 2], jnp.int32)
    own_masks = ((my_x + hops) & 3 ^ my_x) << 1
    met = lambda masks: jnp.any(round_masks[None, :] == masks[:, None], axis=1)
    own_flags = jnp.where(met(own_masks) | (own_masks == 0), 1.0, 0.0).astype(jnp.float32)
    far_masks = own_masks | 1
    far_flags = jnp.where(met(far_masks), 1.0, 0.0).astype(jnp.float32)

    far_images = [
        to_z(rows)
        for rows in staged(
            [(image_embeds, 0, FIRST), (image_embeds, FIRST, pair_rows - FIRST)]
        )
    ]
    text_below = to_x(text_embeds, 1)
    text_above = to_x(text_embeds, -1)
    text_across = [to_x(text_below[:half], 1), to_x(text_above[half:], -1)]
    near_texts = [text_embeds, text_above, text_below]
    all_texts = near_texts + text_across

    near_coefs, grad_near, loss_near = tiles(
        scalars, own_flags[:3], scalars, image_embeds, near_texts, home=True
    )
    first_coefs, first_grad, first_loss = tiles(
        scalars, far_flags, loss_near, far_images[0], all_texts, grad_dtype=jnp.bfloat16
    )
    across_coefs, grad_own, loss_across = tiles(
        scalars, own_flags[3:], first_loss, image_embeds, text_across, earlier=grad_near
    )
    second_coefs, _, second_loss = tiles(
        scalars, far_flags, loss_across, far_images[1], all_texts, grad_dtype=None
    )

    own_coefs = near_coefs + across_coefs
    images = [image_embeds] + far_images
    coefs = [[own_coefs[i], first_coefs[i], second_coefs[i]] for i in range(5)]
    across_low, across_high = text_partials(
        images, [(coefs[3], 0, half), (coefs[4], 0, half)], jnp.bfloat16
    )
    passing_low, passing_high = to_x(across_low, 1), to_x(across_high, -1)
    above_high, below_low = text_partials(
        images, [(coefs[1], half, half), (coefs[2], 0, half)], jnp.bfloat16, after=[across_low]
    )
    from_below_high, from_above_low = to_x(above_high, 1), to_x(below_low, -1)
    second_grad, far_loss = image_partial(
        all_texts, second_coefs, [first_loss, second_loss], [above_high]
    )
    returned = [to_z(first_grad), to_z(second_grad)]
    far_loss = to_z(far_loss)
    image_grad, token = add_rows(grad_own, returned[0], 0, cost=MIDDLE)
    above_low, below_high = text_partials(
        images,
        [(coefs[1], 0, half), (coefs[2], half, half)],
        jnp.bfloat16,
        earlier=[passing_low, passing_high],
        after=[token],
    )
    from_below_low, from_above_high = to_x(above_low, 1), to_x(below_high, -1)
    text_low, text_high, far_loss = text_partials(
        images,
        [(coefs[0], 0, half), (coefs[0], half, half)],
        jnp.float32,
        earlier=[from_above_low, from_below_high],
        passed=[far_loss],
        after=[above_low],
        cost=LARGE,
    )
    text_grad = joined(text_low, text_high, from_below_low, from_above_high)
    image_grad, _ = add_rows(grad_own, returned[1], FIRST, into=image_grad)

    sums = jnp.concatenate([loss_near, loss_across, far_loss])
    masks = jnp.concatenate([own_masks, far_masks])
    wanted = jnp.concatenate([jnp.zeros((1,), jnp.int32), round_masks])
    losses = jnp.sum(jnp.where(wanted[:, None] == masks[None, :], sums[None, :], 0.0), axis=1)
    losses = losses / (pair_rows * pair_rows)
    return (image_grad, text_grad, losses[None, :])


def solution(mesh):
    return jax.shard_map(
        shards,
        mesh=mesh,
        in_specs=(P("dp", None), P("dp", None), P(), P(), P("dp", None)),
        out_specs=(P("dp", None), P("dp", None), P("dp", None)),
        check_vma=False,
    )
```

time: 147 us -> 124 us (0.84)
  the two profiles are of different devices: /device:TPU:48 before, /device:TPU:42 now
where the time goes in v2:
time: 124 us; the launch traced here: 123 us
  waiting for transfers between devices  51.6 us (42%)
  Pallas kernels  34.5 us (28%)
  starting transfers between devices  33.3 us (27%)
  between operations  2.08 us (2%)
  other arithmetic  1.24 us (1%)
    ppermute x5, waiting for transfers between devices, to_z(): lax.ppermute(value, 'dp', [(i, i ^ 1 << Z_BIT) for i in range(count)])  34.4 us
    ppermute x5, starting transfers between devices, to_z(): lax.ppermute(value, 'dp', [(i, i ^ 1 << Z_BIT) for i in range(count)])  22 us
    pallas_call x4, Pallas kernels, tiles(): pl.pallas_call(functools.partial(tiles_kernel, blocks, home, len(extra) >...  18.3 us
    ppermute x10, waiting for transfers between devices, to_x(): lax.ppermute(value, 'dp', [(i, x_neighbour(i, hop)) for i in range(count)])  17.2 us
    ppermute x10, starting transfers between devices, to_x(): lax.ppermute(value, 'dp', [(i, x_neighbour(i, hop)) for i in range(count)])  11.4 us
    pallas_call x4, Pallas kernels, text_partials(): pl.pallas_call(functools.partial(text_kernel, len(images), [(first, rows)...  7.76 us
  transfers between devices with their start and end apart: 15, of which 6 were waited for; matrix products, arithmetic and copies ran while one was open for 1% of the time, Pallas kernels for 27%

profile of v2, /device:TPU:42, one launch (start us, length us, event | category | flops | bytes accessed | tf_op | source)
XLA Modules:
  0.0 122.9 jit_solution(7630896039806188771)
XLA Ops:
  0.7 1.6 %collective-permute-start.1 = (bf16[512,1152]{1,0:T(8,128)(2,1)}, bf16[512,1152]{1,0:T(8,128)(2,1)S(1)}, u32[]{:S(2)}, u32[]{:S(2)}) collective-permute-start(bf16[512,1152]{1,0:T(8,128)(2,1)} %refs_0_.9), channel_id=1, source_target_pairs={{0,64},{1,65},{2,66},{3,67},{4,68},{5,69},{6,70},{7,71},{8,72},{9,... | collective-permute-start | bytes 3538952 | tf_op jit(solution)/shard_map/ppermute | solution.py:31
  2.2 0.5 collective-permute-start
  2.8 2.3 %shard_map.86 = (bf16[256,1152]{1,0:T(8,128)(2,1)}, bf16[256,1152]{1,0:T(8,128)(2,1)}) custom-call(bf16[512,1152]{1,0:T(8,128)(2,1)} %refs_0_.11, bf16[512,1152]{1,0:T(8,128)(2,1)} %refs_0_.11), custom_call_target="tpu_custom_call" | custom-call | flops 1024 | bytes 1024 | tf_op jit(solution)/shard_map/pallas_call | solution.py:56
  5.0 6.4 %collective-permute-start.2 = (bf16[256,1152]{1,0:T(8,128)(2,1)}, bf16[256,1152]{1,0:T(8,128)(2,1)S(1)}, u32[]{:S(2)}, u32[]{:S(2)}) collective-permute-start(bf16[256,1152]{1,0:T(8,128)(2,1)} %get-tuple-element.42), channel_id=1, source_target_pairs={{0,32},{1,33},{2,34},{3,35},{4,36},{5,37},{6,38},{7,39},{8,40},{9,... | collective-permute-start | bytes 1769480 | tf_op jit(solution)/shard_map/ppermute | solution.py:36
  11.6 17.1 %collective-permute-done.1.rest_2_.refs_2_ = bf16[512,1152]{1,0:T(8,128)(2,1)S(1)} collective-permute-done((bf16[512,1152]{1,0:T(8,128)(2,1)}, bf16[512,1152]{1,0:T(8,128)(2,1)S(1)}, u32[]{:S(2)}, u32[]{:S(2)}) %collective-permute-start.1) | collective-permute-done | bytes 1179680 | tf_op jit(solution)/shard_map/ppermute | solution.py:31
  28.7 1.6 %collective-permute-start.3 = (bf16[256,1152]{1,0:T(8,128)(2,1)S(1)}, bf16[256,1152]{1,0:T(8,128)(2,1)S(1)}, u32[]{:S(2)}, u32[]{:S(2)}) collective-permute-start(bf16[256,1152]{1,0:T(8,128)(2,1)S(1)} %slice.16), channel_id=1, source_target_pairs={{0,64},{1,65},{2,66},{3,67},{4,68},{5,69},{6,70},{7,71},{8,72},{9,... | collective-permute-start | bytes 1769480 | tf_op jit(solution)/shard_map/ppermute | solution.py:31
  30.3 0.8 collective-permute-start.4
  32.7 6.4 %shard_map.85 = (bf16[512,512]{1,0:T(8,128)(2,1)S(1)}, bf16[512,512]{1,0:T(8,128)(2,1)S(1)}, bf16[512,512]{1,0:T(8,128)(2,1)S(1)}, f32[512,1152]{1,0:T(8,128)S(1)}, f32[3]{0:T(128)S(1)}) custom-call(f32[2]{0:T(128)S(1)} %pad_maximum_fusion.scalars.after, f32[3]{0:T(128)S(1)} %bitcast.5, f32[2]{0:T(128)S(1)} %pad_maximum_fusion.scalars.after, ...), custom_call_target="tpu_custom_call" | custom-call | flops 1024 | bytes 1024 | tf_op jit(solution)/shard_map/pallas_call | solution.py:147
  39.2 5.2 %collective-permute-done.2.images.refs_1_ = bf16[256,1152]{1,0:T(8,128)(2,1)S(1)} collective-permute-done((bf16[256,1152]{1,0:T(8,128)(2,1)}, bf16[256,1152]{1,0:T(8,128)(2,1)S(1)}, u32[]{:S(2)}, u32[]{:S(2)}) %collective-permute-start.2) | collective-permute-done | bytes 589856 | tf_op jit(solution)/shard_map/ppermute | solution.py:36
  44.5 5.1 %shard_map.87 = (bf16[512,256]{1,0:T(8,128)(2,1)S(1)}, bf16[512,256]{1,0:T(8,128)(2,1)S(1)}, bf16[512,256]{1,0:T(8,128)(2,1)S(1)}, bf16[256,256]{1,0:T(8,128)(2,...) custom-call(f32[2]{0:T(128)S(1)} %pad_maximum_fusion.scalars.after, ...), custom_call_target="tpu_custom_call" | custom-call | flops 1024 | bytes 1024 | tf_op jit(solution)/shard_map/pallas_call | solution.py:147
  49.6 6.6 %collective-permute-start.7 = (bf16[256,1152]{1,0:T(8,128)(2,1)S(1)}, bf16[256,1152]{1,0:T(8,128)(2,1)S(1)}, u32[]{:S(2)}, u32[]{:S(2)}) collective-permute-start(bf16[256,1152]{1,0:T(8,128)(2,1)S(1)} %get-tuple-element.65), channel_id=1, source_target_pairs={{0,32},{1,33},{2,34},{3,35},{4,36},{5,37},{6,38},{7,39},{8,40},{9,... | collective-permute-start | bytes 1769480 | tf_op jit(solution)/shard_map/ppermute | solution.py:36
  56.2 2.8 %shard_map.88 = (bf16[256,512]{1,0:T(8,128)(2,1)S(1)}, bf16[256,512]{1,0:T(8,128)(2,1)S(1)}, f32[512,1152]{1,0:T(8,128)S(1)}, f32[2]{0:T(128)S(1)}) custom-call(f32[2]{0:T(128)S(1)} %pad_maximum_fusion.scalars.after, f32[2]{0:T(128)S(1)} %slice.12.flags, f32[5]{0:T(128)S(1)} %get-tuple-element.43.after.refs_10_, bf16[512,1152]{1,0:T(8,128)(2,1)S(1)} %copy-done, ...), custom_call_target="tpu_custom_call" | custom-call | flops 1024 | bytes 1024 | tf_op jit(solution)/shard_map/pallas_call | solution.py:147
  59.1 11.4 %collective-permute-done.5.images.refs_2_ = bf16[256,1152]{1,0:T(8,128)(2,1)S(1)} collective-permute-done((bf16[256,1152]{1,0:T(8,128)(2,1)}, bf16[256,1152]{1,0:T(8,128)(2,1)S(1)}, u32[]{:S(2)}, u32[]{:S(2)}) %collective-permute-start.5) | collective-permute-done | bytes 589856 | tf_op jit(solution)/shard_map/ppermute | solution.py:36
  70.5 4.0 %shard_map.89 = (bf16[512,256]{1,0:T(8,128)(2,1)S(1)}, bf16[512,256]{1,0:T(8,128)(2,1)S(1)}, bf16[512,256]{1,0:T(8,128)(2,1)S(1)}, bf16[256,256]{1,0:T(8,128)(2,...) custom-call(f32[2]{0:T(128)S(1)} %pad_maximum_fusion.scalars.after, f32[5]{0:T(128)S(1)} %broadcast_select_fusion.flags, ...), custom_call_target="tpu_custom_call" | custom-call | flops 1024 | bytes 1024 | tf_op jit(solution)/shard_map/pallas_call | solution.py:147
  74.5 1.5 %shard_map.90 = (bf16[256,1152]{1,0:T(8,128)(2,1)S(1)}, bf16[256,1152]{1,0:T(8,128)(2,1)S(1)}) custom-call(bf16[512,1152]{1,0:T(8,128)(2,1)S(1)} %copy-done, bf16[256,1152]{1,0:T(8,128)(2,1)S(1)} %collective-permute-done.2.images.refs_1_, bf16[256,1152]{1,0:T(8,128)(2,1)S(1)} %collective-permute-done.5.images.refs_2_, ...), custom_call_target="tpu_custom_call" | custom-call | flops 1024 | bytes 1024 | tf_op jit(solution)/shard_map/pallas_call | solution.py:220
  76.0 2.0 %collective-permute-start.12 = (bf16[256,1152]{1,0:T(8,128)(2,1)S(1)}, bf16[256,1152]{1,0:T(8,128)(2,1)S(1)}, u32[]{:S(2)}, u32[]{:S(2)}) collective-permute-start(bf16[256,1152]{1,0:T(8,128)(2,1)S(1)} %get-tuple-element.72), channel_id=1, source_target_pairs={{0,192},{1,193},{2,194},{3,195},{4,196},{5,197},{6,198},{7,199},{8... | collective-permute-start | bytes 1769480 | tf_op jit(solution)/shard_map/ppermute | solution.py:31
  78.0 0.7 collective-permute-start.11
  78.7 1.5 %shard_map.91 = (bf16[256,1152]{1,0:T(8,128)(2,1)S(1)}, bf16[256,1152]{1,0:T(8,128)(2,1)S(1)}) custom-call(bf16[512,1152]{1,0:T(8,128)(2,1)S(1)} %copy-done, bf16[256,1152]{1,0:T(8,128)(2,1)S(1)} %collective-permute-done.2.images.refs_1_, bf16[256,1152]{1,0:T(8,128)(2,1)S(1)} %collective-permute-done.5.images.refs_2_, ...), custom_call_target="tpu_custom_call" | custom-call | flops 1024 | bytes 1024 | tf_op jit(solution)/shard_map/pallas_call | solution.py:220
  80.3 1.4 %collective-permute-start.8 = (bf16[256,1152]{1,0:T(8,128)(2,1)S(1)}, bf16[256,1152]{1,0:T(8,128)(2,1)S(1)}, u32[]{:S(2)}, u32[]{:S(2)}) collective-permute-start(bf16[256,1152]{1,0:T(8,128)(2,1)S(1)} %get-tuple-element.70), channel_id=1, source_target_pairs={{0,192},{1,193},{2,194},{3,195},{4,196},{5,197},{6,198},{7,199},{8... | collective-permute-start | bytes 1769480 | tf_op jit(solution)/shard_map/ppermute | solution.py:31
  81.7 0.7 collective-permute-start.9
  82.5 2.5 %shard_map.92 = (bf16[256,1152]{1,0:T(8,128)(2,1)S(1)}, f32[5]{0:T(128)S(1)}) custom-call(bf16[512,1152]{1,0:T(8,128)(2,1)S(1)} %copy-done.1, bf16[512,1152]{1,0:T(8,128)(2,1)S(1)} %collective-permute-done.rest_1_.refs_1_, bf16[512,1152]{1,0:T(8,128)(2,1)S(1)} %collective-permute-done.1.rest_2_.refs_2_, ...), custom_call_target="tpu_custom_call" | custom-call | flops 1024 | bytes 1024 | tf_op jit(solution)/shard_map/pallas_call | solution.py:180
  85.0 3.0 %collective-permute-done.7.block = bf16[256,1152]{1,0:T(8,128)(2,1)S(1)} collective-permute-done((bf16[256,1152]{1,0:T(8,128)(2,1)S(1)}, bf16[256,1152]{1,0:T(8,128)(2,1)S(1)}, u32[]{:S(2)}, u32[]{:S(2)}) %collective-permute-start.7) | collective-permute-done | bytes 589856 | tf_op jit(solution)/shard_map/ppermute | solution.py:36
  88.0 5.3 %collective-permute-start.10 = (f32[5]{0:T(128)S(1)}, f32[5]{0:T(128)S(1)}, u32[]{:S(2)}, u32[]{:S(2)}) collective-permute-start(f32[5]{0:T(128)S(1)} %get-tuple-element.71), channel_id=1, source_target_pairs={{0,32},{1,33},{2,34},{3,35},{4,36},{5,37},{6,38},{7,39},{8,40},{9,... | collective-permute-start | bytes 68 | tf_op jit(solution)/shard_map/ppermute | solution.py:36
  93.3 1.1 shard_map.93
  94.4 3.6 %collective-permute-start.6 = (bf16[256,1152]{1,0:T(8,128)(2,1)S(1)}, bf16[256,1152]{1,0:T(8,128)(2,1)S(1)}, u32[]{:S(2)}, u32[]{:S(2)}) collective-permute-start(bf16[256,1152]{1,0:T(8,128)(2,1)S(1)} %get-tuple-element.64), channel_id=1, source_target_pairs={{0,32},{1,33},{2,34},{3,35},{4,36},{5,37},{6,38},{7,39},{8,40},{9,... | collective-permute-start | bytes 1769480 | tf_op jit(solution)/shard_map/ppermute | solution.py:36
  98.0 2.2 %shard_map.95 = (bf16[256,1152]{1,0:T(8,128)(2,1)S(1)}, bf16[256,1152]{1,0:T(8,128)(2,1)S(1)}) custom-call(bf16[512,1152]{1,0:T(8,128)(2,1)S(1)} %copy-done, bf16[256,1152]{1,0:T(8,128)(2,1)S(1)} %collective-permute-done.2.images.refs_1_, bf16[256,1152]{1,0:T(8,128)(2,1)S(1)} %collective-permute-done.5.images.refs_2_, ...), custom_call_target="tpu_custom_call" | custom-call | flops 1024 | bytes 1024 | tf_op jit(solution)/shard_map/pallas_call | solution.py:220
  100.2 1.4 %collective-permute-start.14 = (bf16[256,1152]{1,0:T(8,128)(2,1)S(1)}, bf16[256,1152]{1,0:T(8,128)(2,1)S(1)}, u32[]{:S(2)}, u32[]{:S(2)}) collective-permute-start(bf16[256,1152]{1,0:T(8,128)(2,1)S(1)} %get-tuple-element.77), channel_id=1, source_target_pairs={{0,192},{1,193},{2,194},{3,195},{4,196},{5,197},{6,198},{7,199},{8... | collective-permute-start | bytes 1769480 | tf_op jit(solution)/shard_map/ppermute | solution.py:31
  101.6 0.7 collective-permute-start.13
  102.3 2.5 %shard_map.96 = (f32[256,1152]{1,0:T(8,128)S(1)}, f32[256,1152]{1,0:T(8,128)S(1)}, f32[5]{0:T(128)S(1)}) custom-call(bf16[512,1152]{1,0:T(8,128)(2,1)S(1)} %copy-done, bf16[256,1152]{1,0:T(8,128)(2,1)S(1)} %collective-permute-done.2.images.refs_1_, bf16[256,1152]{1,0:T(8,128)(2,1)S(1)} %collective-permute-done.5.images.refs_2_, ...), custom_call_target="tpu_custom_call" | custom-call | flops 17179869184 | bytes 1048576 | tf_op jit(solution)/shard_map/pallas_call | solution.py:220
  104.8 14.8 %collective-permute-done.6.block = bf16[256,1152]{1,0:T(8,128)(2,1)S(1)} collective-permute-done((bf16[256,1152]{1,0:T(8,128)(2,1)S(1)}, bf16[256,1152]{1,0:T(8,128)(2,1)S(1)}, u32[]{:S(2)}, u32[]{:S(2)}) %collective-permute-start.6) | collective-permute-done | bytes 589856 | tf_op jit(solution)/shard_map/ppermute | solution.py:36
  119.6 1.1 shard_map.94
  121.4 1.5 %shard_map.97 = f32[512,1152]{1,0:T(8,128)} custom-call(f32[256,1152]{1,0:T(8,128)S(1)} %get-tuple-element.75.low, f32[256,1152]{1,0:T(8,128)S(1)} %get-tuple-element.76.high, bf16[256,1152]{1,0:T(8,128)(2,1)S(1)} %collective-permute-done.13.low_more, bf16[256,1152]{1,0:T(8,128)(2,1)S(1)} %collective-permute-done.14.high_more), custom_call_target="tpu_custom_call" | custom-call | flops 1024 | bytes 1024 | tf_op jit(solution)/shard_map/pallas_call | solution.py:279
  (33 shorter events, 1.7 us)
Async XLA Ops:
  0.6 10.9 %copy-start.2 = (s32[5]{0:T(128)S(1)}, s32[5]{0:T(128)}, u32[]{:S(2)}) copy-start(s32[5]{0:T(128)} %constant.27.clone) | copy-start | bytes 64
  0.6 10.9 %copy-start.3 = (s32[1,6]{1,0:T(1,128)S(1)}, s32[1,6]{1,0:T(1,128)}, u32[]{:S(2)}) copy-start(s32[1,6]{1,0:T(1,128)} %param.10) | copy-start | bytes 76
  0.7 28.0 %collective-permute-start.1 = (bf16[512,1152]{1,0:T(8,128)(2,1)}, bf16[512,1152]{1,0:T(8,128)(2,1)S(1)}, u32[]{:S(2)}, u32[]{:S(2)}) collective-permute-start(bf16[512,1152]{1,0:T(8,128)(2,1)} %refs_0_.9), channel_id=1, source_target_pairs={{0,64},{1,65},{2,66},{3,67},{4,68},{5,69},{6,70},{7,71},{8,72},{9,... | collective-permute-start | bytes 3538952 | tf_op jit(solution)/shard_map/ppermute | solution.py:31
  2.2 28.0 %collective-permute-start = (bf16[512,1152]{1,0:T(8,128)(2,1)}, bf16[512,1152]{1,0:T(8,128)(2,1)S(1)}, u32[]{:S(2)}, u32[]{:S(2)}) collective-permute-start(bf16[512,1152]{1,0:T(8,128)(2,1)} %refs_0_.9), channel_id=1, source_target_pairs={{0,192},{1,193},{2,194},{3,195},{4,196},{5,197},{6,198},{7,199},{8... | collective-permute-start | bytes 3538952 | tf_op jit(solution)/shard_map/ppermute | solution.py:31
  5.0 39.3 %collective-permute-start.2 = (bf16[256,1152]{1,0:T(8,128)(2,1)}, bf16[256,1152]{1,0:T(8,128)(2,1)S(1)}, u32[]{:S(2)}, u32[]{:S(2)}) collective-permute-start(bf16[256,1152]{1,0:T(8,128)(2,1)} %get-tuple-element.42), channel_id=1, source_target_pairs={{0,32},{1,33},{2,34},{3,35},{4,36},{5,37},{6,38},{7,39},{8,40},{9,... | collective-permute-start | bytes 1769480 | tf_op jit(solution)/shard_map/ppermute | solution.py:36
  11.4 59.1 %collective-permute-start.5 = (bf16[256,1152]{1,0:T(8,128)(2,1)}, bf16[256,1152]{1,0:T(8,128)(2,1)S(1)}, u32[]{:S(2)}, u32[]{:S(2)}) collective-permute-start(bf16[256,1152]{1,0:T(8,128)(2,1)} %get-tuple-element.47), channel_id=1, source_target_pairs={{0,32},{1,33},{2,34},{3,35},{4,36},{5,37},{6,38},{7,39},{8,40},{9,... | collective-permute-start | bytes 1769480 | tf_op jit(solution)/shard_map/ppermute | solution.py:36
  11.5 21.2 %copy-start = (bf16[512,1152]{1,0:T(8,128)(2,1)S(1)}, bf16[512,1152]{1,0:T(8,128)(2,1)}, u32[]{:S(2)}) copy-start(bf16[512,1152]{1,0:T(8,128)(2,1)} %refs_0_.11) | copy-start | bytes 3538948
  11.5 21.2 %copy-start.1 = (bf16[512,1152]{1,0:T(8,128)(2,1)S(1)}, bf16[512,1152]{1,0:T(8,128)(2,1)}, u32[]{:S(2)}) copy-start(bf16[512,1152]{1,0:T(8,128)(2,1)} %refs_0_.9) | copy-start | bytes 3538948
  28.7 15.7 %collective-permute-start.3 = (bf16[256,1152]{1,0:T(8,128)(2,1)S(1)}, bf16[256,1152]{1,0:T(8,128)(2,1)S(1)}, u32[]{:S(2)}, u32[]{:S(2)}) collective-permute-start(bf16[256,1152]{1,0:T(8,128)(2,1)S(1)} %slice.16), channel_id=1, source_target_pairs={{0,64},{1,65},{2,66},{3,67},{4,68},{5,69},{6,70},{7,71},{8,72},{9,... | collective-permute-start | bytes 1769480 | tf_op jit(solution)/shard_map/ppermute | solution.py:31
  30.3 14.2 %collective-permute-start.4 = (bf16[256,1152]{1,0:T(8,128)(2,1)S(1)}, bf16[256,1152]{1,0:T(8,128)(2,1)S(1)}, u32[]{:S(2)}, u32[]{:S(2)}) collective-permute-start(bf16[256,1152]{1,0:T(8,128)(2,1)S(1)} %slice.17), channel_id=1, source_target_pairs={{0,192},{1,193},{2,194},{3,195},{4,196},{5,197},{6,198},{7,199},{8... | collective-permute-start | bytes 1769480 | tf_op jit(solution)/shard_map/ppermute | solution.py:31
  49.6 38.4 %collective-permute-start.7 = (bf16[256,1152]{1,0:T(8,128)(2,1)S(1)}, bf16[256,1152]{1,0:T(8,128)(2,1)S(1)}, u32[]{:S(2)}, u32[]{:S(2)}) collective-permute-start(bf16[256,1152]{1,0:T(8,128)(2,1)S(1)} %get-tuple-element.65), channel_id=1, source_target_pairs={{0,32},{1,33},{2,34},{3,35},{4,36},{5,37},{6,38},{7,39},{8,40},{9,... | collective-permute-start | bytes 1769480 | tf_op jit(solution)/shard_map/ppermute | solution.py:36
  76.0 18.3 %collective-permute-start.12 = (bf16[256,1152]{1,0:T(8,128)(2,1)S(1)}, bf16[256,1152]{1,0:T(8,128)(2,1)S(1)}, u32[]{:S(2)}, u32[]{:S(2)}) collective-permute-start(bf16[256,1152]{1,0:T(8,128)(2,1)S(1)} %get-tuple-element.72), channel_id=1, source_target_pairs={{0,192},{1,193},{2,194},{3,195},{4,196},{5,197},{6,198},{7,199},{8... | collective-permute-start | bytes 1769480 | tf_op jit(solution)/shard_map/ppermute | solution.py:31
  78.0 20.0 %collective-permute-start.11 = (bf16[256,1152]{1,0:T(8,128)(2,1)S(1)}, bf16[256,1152]{1,0:T(8,128)(2,1)S(1)}, u32[]{:S(2)}, u32[]{:S(2)}) collective-permute-start(bf16[256,1152]{1,0:T(8,128)(2,1)S(1)} %get-tuple-element.62.refs_9_), channel_id=1, source_target_pairs={{0,64},{1,65},{2,66},{3,67},{4,68},{5,69},{6,70},{7,71},{8,72},{9,... | collective-permute-start | bytes 1769480 | tf_op jit(solution)/shard_map/ppermute | solution.py:31
  80.3 22.0 %collective-permute-start.8 = (bf16[256,1152]{1,0:T(8,128)(2,1)S(1)}, bf16[256,1152]{1,0:T(8,128)(2,1)S(1)}, u32[]{:S(2)}, u32[]{:S(2)}) collective-permute-start(bf16[256,1152]{1,0:T(8,128)(2,1)S(1)} %get-tuple-element.70), channel_id=1, source_target_pairs={{0,192},{1,193},{2,194},{3,195},{4,196},{5,197},{6,198},{7,199},{8... | collective-permute-start | bytes 1769480 | tf_op jit(solution)/shard_map/ppermute | solution.py:31
  81.7 20.6 %collective-permute-start.9 = (bf16[256,1152]{1,0:T(8,128)(2,1)S(1)}, bf16[256,1152]{1,0:T(8,128)(2,1)S(1)}, u32[]{:S(2)}, u32[]{:S(2)}) collective-permute-start(bf16[256,1152]{1,0:T(8,128)(2,1)S(1)} %get-tuple-element.63.refs_12_), channel_id=1, source_target_pairs={{0,64},{1,65},{2,66},{3,67},{4,68},{5,69},{6,70},{7,71},{8,72},{9,... | collective-permute-start | bytes 1769480 | tf_op jit(solution)/shard_map/ppermute | solution.py:31
  88.0 13.6 %collective-permute-start.10 = (f32[5]{0:T(128)S(1)}, f32[5]{0:T(128)S(1)}, u32[]{:S(2)}, u32[]{:S(2)}) collective-permute-start(f32[5]{0:T(128)S(1)} %get-tuple-element.71), channel_id=1, source_target_pairs={{0,32},{1,33},{2,34},{3,35},{4,36},{5,37},{6,38},{7,39},{8,40},{9,... | collective-permute-start | bytes 68 | tf_op jit(solution)/shard_map/ppermute | solution.py:36
  94.4 25.2 %collective-permute-start.6 = (bf16[256,1152]{1,0:T(8,128)(2,1)S(1)}, bf16[256,1152]{1,0:T(8,128)(2,1)S(1)}, u32[]{:S(2)}, u32[]{:S(2)}) collective-permute-start(bf16[256,1152]{1,0:T(8,128)(2,1)S(1)} %get-tuple-element.64), channel_id=1, source_target_pairs={{0,32},{1,33},{2,34},{3,35},{4,36},{5,37},{6,38},{7,39},{8,40},{9,... | collective-permute-start | bytes 1769480 | tf_op jit(solution)/shard_map/ppermute | solution.py:36
  100.2 21.2 %collective-permute-start.14 = (bf16[256,1152]{1,0:T(8,128)(2,1)S(1)}, bf16[256,1152]{1,0:T(8,128)(2,1)S(1)}, u32[]{:S(2)}, u32[]{:S(2)}) collective-permute-start(bf16[256,1152]{1,0:T(8,128)(2,1)S(1)} %get-tuple-element.77), channel_id=1, source_target_pairs={{0,192},{1,193},{2,194},{3,195},{4,196},{5,197},{6,198},{7,199},{8... | collective-permute-start | bytes 1769480 | tf_op jit(solution)/shard_map/ppermute | solution.py:31
  101.6 19.8 %collective-permute-start.13 = (bf16[256,1152]{1,0:T(8,128)(2,1)S(1)}, bf16[256,1152]{1,0:T(8,128)(2,1)S(1)}, u32[]{:S(2)}, u32[]{:S(2)}) collective-permute-start(bf16[256,1152]{1,0:T(8,128)(2,1)S(1)} %get-tuple-element.74.refs_12_), channel_id=1, source_target_pairs={{0,64},{1,65},{2,66},{3,67},{4,68},{5,69},{6,70},{7,71},{8,72},{9,... | collective-permute-start | bytes 1769480 | tf_op jit(solution)/shard_map/ppermute | solution.py:31

commit v3 on v2

--- a/solution.py
+++ b/solution.py
@@ -362,6 +362,7 @@
         cost=LARGE,
     )
     text_grad = joined(text_low, text_high, from_below_low, from_above_high)
+    grad_own, text_grad = lax.optimization_barrier((grad_own, text_grad))
     image_grad, _ = add_rows(grad_own, returned[1], FIRST, into=image_grad)
 
     sums = jnp.concatenate([loss_near, loss_across, far_loss])

time: 124 us -> 123 us (level); the launches traced: 123 us -> 121 us
  waiting for transfers between devices: 51.6 us -> 49.3 us
    ppermute x5, waiting for transfers between devices: 34.4 us -> 25 us  [to_z(): lax.ppermute(value, 'dp', [(i, i ^ 1 << Z_BIT) for i in range(count)])]
    ppermute x10, waiting for transfers between devices: 17.2 us -> 24.3 us  [to_x(): lax.ppermute(value, 'dp', [(i, x_neighbour(i, hop)) for i in range(count)])]
  transfers between devices with their start and end apart: 15 -> 15, of which waited for: 6 -> 8; matrix products, arithmetic and copies ran while one was open for 1% -> 1% of each run, Pallas kernels for 27% -> 28%
where the time goes in v3:
time: 123 us; the launch traced here: 121 us
  waiting for transfers between devices  49.3 us (40%)
  Pallas kernels  34.5 us (28%)
  starting transfers between devices  33.3 us (27%)
  between operations  2.08 us (2%)
  other arithmetic  1.24 us (1%)
    ppermute x5, waiting for transfers between devices, to_z(): lax.ppermute(value, 'dp', [(i, i ^ 1 << Z_BIT) for i in range(count)])  25 us
    ppermute x10, waiting for transfers between devices, to_x(): lax.ppermute(value, 'dp', [(i, x_neighbour(i, hop)) for i in range(count)])  24.3 us
    ppermute x5, starting transfers between devices, to_z(): lax.ppermute(value, 'dp', [(i, i ^ 1 << Z_BIT) for i in range(count)])  22 us
    pallas_call x4, Pallas kernels, tiles(): pl.pallas_call(functools.partial(tiles_kernel, blocks, home, len(extra) >...  18.3 us
    ppermute x10, starting transfers between devices, to_x(): lax.ppermute(value, 'dp', [(i, x_neighbour(i, hop)) for i in range(count)])  11.4 us
    pallas_call x4, Pallas kernels, text_partials(): pl.pallas_call(functools.partial(text_kernel, len(images), [(first, rows)...  7.76 us
    pallas_call x1, Pallas kernels, image_partial(): pl.pallas_call(functools.partial(image_grad_kernel, blocks), out_shape=[j...  2.46 us
  transfers between devices with their start and end apart: 15, of which 8 were waited for; matrix products, arithmetic and copies ran while one was open for 1% of the time, Pallas kernels for 28%

profile of v3, /device:TPU:42, one launch (start us, length us, event | category | flops | bytes accessed | tf_op | source)
XLA Modules:
  0.0 120.6 jit_solution(7878765591515461055)
XLA Ops:
  0.7 1.6 %collective-permute-start.1 = (bf16[512,1152]{1,0:T(8,128)(2,1)}, bf16[512,1152]{1,0:T(8,128)(2,1)S(1)}, u32[]{:S(2)}, u32[]{:S(2)}) collective-permute-start(bf16[512,1152]{1,0:T(8,128)(2,1)} %refs_0_.9), channel_id=1, source_target_pairs={{0,64},{1,65},{2,66},{3,67},{4,68},{5,69},{6,70},{7,71},{8,72},{9,... | collective-permute-start | bytes 3538952 | tf_op jit(solution)/shard_map/ppermute | solution.py:31
  2.8 2.3 %shard_map.86 = (bf16[256,1152]{1,0:T(8,128)(2,1)}, bf16[256,1152]{1,0:T(8,128)(2,1)}) custom-call(bf16[512,1152]{1,0:T(8,128)(2,1)} %refs_0_.11, bf16[512,1152]{1,0:T(8,128)(2,1)} %refs_0_.11), custom_call_target="tpu_custom_call" | custom-call | flops 1024 | bytes 1024 | tf_op jit(solution)/shard_map/pallas_call | solution.py:56
  5.0 6.4 %collective-permute-start.2 = (bf16[256,1152]{1,0:T(8,128)(2,1)}, bf16[256,1152]{1,0:T(8,128)(2,1)S(1)}, u32[]{:S(2)}, u32[]{:S(2)}) collective-permute-start(bf16[256,1152]{1,0:T(8,128)(2,1)} %get-tuple-element.44), channel_id=1, source_target_pairs={{0,32},{1,33},{2,34},{3,35},{4,36},{5,37},{6,38},{7,39},{8,40},{9,... | collective-permute-start | bytes 1769480 | tf_op jit(solution)/shard_map/ppermute | solution.py:36
  11.6 17.1 %collective-permute-done.1.rest_2_.refs_2_ = bf16[512,1152]{1,0:T(8,128)(2,1)S(1)} collective-permute-done((bf16[512,1152]{1,0:T(8,128)(2,1)}, bf16[512,1152]{1,0:T(8,128)(2,1)S(1)}, u32[]{:S(2)}, u32[]{:S(2)}) %collective-permute-start.1) | collective-permute-done | bytes 1179680 | tf_op jit(solution)/shard_map/ppermute | solution.py:31
  28.7 1.6 %collective-permute-start.3 = (bf16[256,1152]{1,0:T(8,128)(2,1)S(1)}, bf16[256,1152]{1,0:T(8,128)(2,1)S(1)}, u32[]{:S(2)}, u32[]{:S(2)}) collective-permute-start(bf16[256,1152]{1,0:T(8,128)(2,1)S(1)} %slice.16), channel_id=1, source_target_pairs={{0,64},{1,65},{2,66},{3,67},{4,68},{5,69},{6,70},{7,71},{8,72},{9,... | collective-permute-start | bytes 1769480 | tf_op jit(solution)/shard_map/ppermute | solution.py:31
  30.3 0.8 collective-permute-start.4
  32.7 6.4 %shard_map.85 = (bf16[512,512]{1,0:T(8,128)(2,1)S(1)}, bf16[512,512]{1,0:T(8,128)(2,1)S(1)}, bf16[512,512]{1,0:T(8,128)(2,1)S(1)}, f32[512,1152]{1,0:T(8,128)S(1)}, f32[3]{0:T(128)S(1)}) custom-call(f32[2]{0:T(128)S(1)} %pad_maximum_fusion.scalars.after, f32[3]{0:T(128)S(1)} %bitcast.5, f32[2]{0:T(128)S(1)} %pad_maximum_fusion.scalars.after, ...), custom_call_target="tpu_custom_call" | custom-call | flops 1024 | bytes 1024 | tf_op jit(solution)/shard_map/pallas_call | solution.py:147
  39.2 5.2 %collective-permute-done.2.images.refs_1_ = bf16[256,1152]{1,0:T(8,128)(2,1)S(1)} collective-permute-done((bf16[256,1152]{1,0:T(8,128)(2,1)}, bf16[256,1152]{1,0:T(8,128)(2,1)S(1)}, u32[]{:S(2)}, u32[]{:S(2)}) %collective-permute-start.2) | collective-permute-done | bytes 589856 | tf_op jit(solution)/shard_map/ppermute | solution.py:36
  44.5 5.1 %shard_map.87 = (bf16[512,256]{1,0:T(8,128)(2,1)S(1)}, bf16[512,256]{1,0:T(8,128)(2,1)S(1)}, bf16[512,256]{1,0:T(8,128)(2,1)S(1)}, bf16[256,256]{1,0:T(8,128)(2,...) custom-call(f32[2]{0:T(128)S(1)} %pad_maximum_fusion.scalars.after, ...), custom_call_target="tpu_custom_call" | custom-call | flops 1024 | bytes 1024 | tf_op jit(solution)/shard_map/pallas_call | solution.py:147
  49.6 6.6 %collective-permute-start.11 = (bf16[256,1152]{1,0:T(8,128)(2,1)S(1)}, bf16[256,1152]{1,0:T(8,128)(2,1)S(1)}, u32[]{:S(2)}, u32[]{:S(2)}) collective-permute-start(bf16[256,1152]{1,0:T(8,128)(2,1)S(1)} %get-tuple-element.71), channel_id=1, source_target_pairs={{0,32},{1,33},{2,34},{3,35},{4,36},{5,37},{6,38},{7,39},{8,40},{9,... | collective-permute-start | bytes 1769480 | tf_op jit(solution)/shard_map/ppermute | solution.py:36
  56.2 2.8 %shard_map.88 = (bf16[256,512]{1,0:T(8,128)(2,1)S(1)}, bf16[256,512]{1,0:T(8,128)(2,1)S(1)}, f32[512,1152]{1,0:T(8,128)S(1)}, f32[2]{0:T(128)S(1)}) custom-call(f32[2]{0:T(128)S(1)} %pad_maximum_fusion.scalars.after, f32[2]{0:T(128)S(1)} %slice.12.flags, f32[5]{0:T(128)S(1)} %get-tuple-element.45.after.refs_10_, bf16[512,1152]{1,0:T(8,128)(2,1)S(1)} %copy-done, ...), custom_call_target="tpu_custom_call" | custom-call | flops 1024 | bytes 1024 | tf_op jit(solution)/shard_map/pallas_call | solution.py:147
  59.1 11.4 %collective-permute-done.5.images.refs_2_ = bf16[256,1152]{1,0:T(8,128)(2,1)S(1)} collective-permute-done((bf16[256,1152]{1,0:T(8,128)(2,1)}, bf16[256,1152]{1,0:T(8,128)(2,1)S(1)}, u32[]{:S(2)}, u32[]{:S(2)}) %collective-permute-start.5) | collective-permute-done | bytes 589856 | tf_op jit(solution)/shard_map/ppermute | solution.py:36
  70.5 4.0 %shard_map.89 = (bf16[512,256]{1,0:T(8,128)(2,1)S(1)}, bf16[512,256]{1,0:T(8,128)(2,1)S(1)}, bf16[512,256]{1,0:T(8,128)(2,1)S(1)}, bf16[256,256]{1,0:T(8,128)(2,...) custom-call(f32[2]{0:T(128)S(1)} %pad_maximum_fusion.scalars.after, f32[5]{0:T(128)S(1)} %broadcast_select_fusion.flags, ...), custom_call_target="tpu_custom_call" | custom-call | flops 1024 | bytes 1024 | tf_op jit(solution)/shard_map/pallas_call | solution.py:147
  74.5 1.5 %shard_map.90 = (bf16[256,1152]{1,0:T(8,128)(2,1)S(1)}, bf16[256,1152]{1,0:T(8,128)(2,1)S(1)}) custom-call(bf16[512,1152]{1,0:T(8,128)(2,1)S(1)} %copy-done, bf16[256,1152]{1,0:T(8,128)(2,1)S(1)} %collective-permute-done.2.images.refs_1_, bf16[256,1152]{1,0:T(8,128)(2,1)S(1)} %collective-permute-done.5.images.refs_2_, ...), custom_call_target="tpu_custom_call" | custom-call | flops 1024 | bytes 1024 | tf_op jit(solution)/shard_map/pallas_call | solution.py:220
  76.0 2.0 %collective-permute-start.10 = (bf16[256,1152]{1,0:T(8,128)(2,1)S(1)}, bf16[256,1152]{1,0:T(8,128)(2,1)S(1)}, u32[]{:S(2)}, u32[]{:S(2)}) collective-permute-start(bf16[256,1152]{1,0:T(8,128)(2,1)S(1)} %get-tuple-element.70), channel_id=1, source_target_pairs={{0,192},{1,193},{2,194},{3,195},{4,196},{5,197},{6,198},{7,199},{8... | collective-permute-start | bytes 1769480 | tf_op jit(solution)/shard_map/ppermute | solution.py:31
  78.0 0.7 collective-permute-start.9
  78.7 1.5 %shard_map.91 = (bf16[256,1152]{1,0:T(8,128)(2,1)S(1)}, bf16[256,1152]{1,0:T(8,128)(2,1)S(1)}) custom-call(bf16[512,1152]{1,0:T(8,128)(2,1)S(1)} %copy-done, bf16[256,1152]{1,0:T(8,128)(2,1)S(1)} %collective-permute-done.2.images.refs_1_, bf16[256,1152]{1,0:T(8,128)(2,1)S(1)} %collective-permute-done.5.images.refs_2_, ...), custom_call_target="tpu_custom_call" | custom-call | flops 1024 | bytes 1024 | tf_op jit(solution)/shard_map/pallas_call | solution.py:220
  80.3 1.4 %collective-permute-start.6 = (bf16[256,1152]{1,0:T(8,128)(2,1)S(1)}, bf16[256,1152]{1,0:T(8,128)(2,1)S(1)}, u32[]{:S(2)}, u32[]{:S(2)}) collective-permute-start(bf16[256,1152]{1,0:T(8,128)(2,1)S(1)} %get-tuple-element.66), channel_id=1, source_target_pairs={{0,192},{1,193},{2,194},{3,195},{4,196},{5,197},{6,198},{7,199},{8... | collective-permute-start | bytes 1769480 | tf_op jit(solution)/shard_map/ppermute | solution.py:31
  81.7 0.7 collective-permute-start.7
  82.5 2.5 %shard_map.92 = (bf16[256,1152]{1,0:T(8,128)(2,1)S(1)}, f32[5]{0:T(128)S(1)}) custom-call(bf16[512,1152]{1,0:T(8,128)(2,1)S(1)} %copy-done.1, bf16[512,1152]{1,0:T(8,128)(2,1)S(1)} %collective-permute-done.rest_1_.refs_1_, bf16[512,1152]{1,0:T(8,128)(2,1)S(1)} %collective-permute-done.1.rest_2_.refs_2_, ...), custom_call_target="tpu_custom_call" | custom-call | flops 1024 | bytes 1024 | tf_op jit(solution)/shard_map/pallas_call | solution.py:180
  85.0 3.0 %collective-permute-done.11.block = bf16[256,1152]{1,0:T(8,128)(2,1)S(1)} collective-permute-done((bf16[256,1152]{1,0:T(8,128)(2,1)S(1)}, bf16[256,1152]{1,0:T(8,128)(2,1)S(1)}, u32[]{:S(2)}, u32[]{:S(2)}) %collective-permute-start.11) | collective-permute-done | bytes 589856 | tf_op jit(solution)/shard_map/ppermute | solution.py:36
  88.0 5.3 %collective-permute-start.8 = (f32[5]{0:T(128)S(1)}, f32[5]{0:T(128)S(1)}, u32[]{:S(2)}, u32[]{:S(2)}) collective-permute-start(f32[5]{0:T(128)S(1)} %get-tuple-element.69), channel_id=1, source_target_pairs={{0,32},{1,33},{2,34},{3,35},{4,36},{5,37},{6,38},{7,39},{8,40},{9,... | collective-permute-start | bytes 68 | tf_op jit(solution)/shard_map/ppermute | solution.py:36
  93.3 1.1 shard_map.93
  94.4 3.6 %collective-permute-start.14 = (bf16[256,1152]{1,0:T(8,128)(2,1)S(1)}, bf16[256,1152]{1,0:T(8,128)(2,1)S(1)}, u32[]{:S(2)}, u32[]{:S(2)}) collective-permute-start(bf16[256,1152]{1,0:T(8,128)(2,1)S(1)} %get-tuple-element.78), channel_id=1, source_target_pairs={{0,32},{1,33},{2,34},{3,35},{4,36},{5,37},{6,38},{7,39},{8,40},{9,... | collective-permute-start | bytes 1769480 | tf_op jit(solution)/shard_map/ppermute | solution.py:36
  98.0 2.2 %shard_map.94 = (bf16[256,1152]{1,0:T(8,128)(2,1)S(1)}, bf16[256,1152]{1,0:T(8,128)(2,1)S(1)}) custom-call(bf16[512,1152]{1,0:T(8,128)(2,1)S(1)} %copy-done, bf16[256,1152]{1,0:T(8,128)(2,1)S(1)} %collective-permute-done.2.images.refs_1_, bf16[256,1152]{1,0:T(8,128)(2,1)S(1)} %collective-permute-done.5.images.refs_2_, ...), custom_call_target="tpu_custom_call" | custom-call | flops 1024 | bytes 1024 | tf_op jit(solution)/shard_map/pallas_call | solution.py:220
  100.2 1.4 %collective-permute-start.13 = (bf16[256,1152]{1,0:T(8,128)(2,1)S(1)}, bf16[256,1152]{1,0:T(8,128)(2,1)S(1)}, u32[]{:S(2)}, u32[]{:S(2)}) collective-permute-start(bf16[256,1152]{1,0:T(8,128)(2,1)S(1)} %get-tuple-element.76), channel_id=1, source_target_pairs={{0,192},{1,193},{2,194},{3,195},{4,196},{5,197},{6,198},{7,199},{8... | collective-permute-start | bytes 1769480 | tf_op jit(solution)/shard_map/ppermute | solution.py:31
  102.3 2.5 %shard_map.95 = (f32[256,1152]{1,0:T(8,128)S(1)}, f32[256,1152]{1,0:T(8,128)S(1)}, f32[5]{0:T(128)S(1)}) custom-call(bf16[512,1152]{1,0:T(8,128)(2,1)S(1)} %copy-done, bf16[256,1152]{1,0:T(8,128)(2,1)S(1)} %collective-permute-done.2.images.refs_1_, bf16[256,1152]{1,0:T(8,128)(2,1)S(1)} %collective-permute-done.5.images.refs_2_, ...), custom_call_target="tpu_custom_call" | custom-call | flops 17179869184 | bytes 1048576 | tf_op jit(solution)/shard_map/pallas_call | solution.py:220
  105.5 6.0 %collective-permute-done.13.high_more = bf16[256,1152]{1,0:T(8,128)(2,1)S(1)} collective-permute-done((bf16[256,1152]{1,0:T(8,128)(2,1)S(1)}, bf16[256,1152]{1,0:T(8,128)(2,1)S(1)}, u32[]{:S(2)}, u32[]{:S(2)}) %collective-permute-start.13) | collective-permute-done | bytes 589856 | tf_op jit(solution)/shard_map/ppermute | solution.py:31
  111.6 1.0 collective-permute-done.12.low_more
  112.6 1.5 %shard_map.96 = f32[512,1152]{1,0:T(8,128)} custom-call(f32[256,1152]{1,0:T(8,128)S(1)} %get-tuple-element.74.low, f32[256,1152]{1,0:T(8,128)S(1)} %get-tuple-element.75.high, bf16[256,1152]{1,0:T(8,128)(2,1)S(1)} %collective-permute-done.12.low_more, bf16[256,1152]{1,0:T(8,128)(2,1)S(1)} %collective-permute-done.13.high_more), custom_call_target="tpu_custom_call" | custom-call | flops 1024 | bytes 1024 | tf_op jit(solution)/shard_map/pallas_call | solution.py:279
  114.1 5.4 %collective-permute-done.14.block = bf16[256,1152]{1,0:T(8,128)(2,1)S(1)} collective-permute-done((bf16[256,1152]{1,0:T(8,128)(2,1)S(1)}, bf16[256,1152]{1,0:T(8,128)(2,1)S(1)}, u32[]{:S(2)}, u32[]{:S(2)}) %collective-permute-start.14) | collective-permute-done | bytes 589856 | tf_op jit(solution)/shard_map/ppermute | solution.py:36
  119.6 1.1 shard_map.97
  (33 shorter events, 2.9 us)
Async XLA Ops:
  0.6 10.9 %copy-start.2 = (s32[5]{0:T(128)S(1)}, s32[5]{0:T(128)}, u32[]{:S(2)}) copy-start(s32[5]{0:T(128)} %constant.27.clone) | copy-start | bytes 64
  0.6 10.9 %copy-start.3 = (s32[1,6]{1,0:T(1,128)S(1)}, s32[1,6]{1,0:T(1,128)}, u32[]{:S(2)}) copy-start(s32[1,6]{1,0:T(1,128)} %param.10) | copy-start | bytes 76
  0.7 28.0 %collective-permute-start.1 = (bf16[512,1152]{1,0:T(8,128)(2,1)}, bf16[512,1152]{1,0:T(8,128)(2,1)S(1)}, u32[]{:S(2)}, u32[]{:S(2)}) collective-permute-start(bf16[512,1152]{1,0:T(8,128)(2,1)} %refs_0_.9), channel_id=1, source_target_pairs={{0,64},{1,65},{2,66},{3,67},{4,68},{5,69},{6,70},{7,71},{8,72},{9,... | collective-permute-start | bytes 3538952 | tf_op jit(solution)/shard_map/ppermute | solution.py:31
  2.2 28.0 %collective-permute-start = (bf16[512,1152]{1,0:T(8,128)(2,1)}, bf16[512,1152]{1,0:T(8,128)(2,1)S(1)}, u32[]{:S(2)}, u32[]{:S(2)}) collective-permute-start(bf16[512,1152]{1,0:T(8,128)(2,1)} %refs_0_.9), channel_id=1, source_target_pairs={{0,192},{1,193},{2,194},{3,195},{4,196},{5,197},{6,198},{7,199},{8... | collective-permute-start | bytes 3538952 | tf_op jit(solution)/shard_map/ppermute | solution.py:31
  5.0 39.3 %collective-permute-start.2 = (bf16[256,1152]{1,0:T(8,128)(2,1)}, bf16[256,1152]{1,0:T(8,128)(2,1)S(1)}, u32[]{:S(2)}, u32[]{:S(2)}) collective-permute-start(bf16[256,1152]{1,0:T(8,128)(2,1)} %get-tuple-element.44), channel_id=1, source_target_pairs={{0,32},{1,33},{2,34},{3,35},{4,36},{5,37},{6,38},{7,39},{8,40},{9,... | collective-permute-start | bytes 1769480 | tf_op jit(solution)/shard_map/ppermute | solution.py:36
  11.4 59.1 %collective-permute-start.5 = (bf16[256,1152]{1,0:T(8,128)(2,1)}, bf16[256,1152]{1,0:T(8,128)(2,1)S(1)}, u32[]{:S(2)}, u32[]{:S(2)}) collective-permute-start(bf16[256,1152]{1,0:T(8,128)(2,1)} %get-tuple-element.48), channel_id=1, source_target_pairs={{0,32},{1,33},{2,34},{3,35},{4,36},{5,37},{6,38},{7,39},{8,40},{9,... | collective-permute-start | bytes 1769480 | tf_op jit(solution)/shard_map/ppermute | solution.py:36
  11.5 21.2 %copy-start = (bf16[512,1152]{1,0:T(8,128)(2,1)S(1)}, bf16[512,1152]{1,0:T(8,128)(2,1)}, u32[]{:S(2)}) copy-start(bf16[512,1152]{1,0:T(8,128)(2,1)} %refs_0_.11) | copy-start | bytes 3538948
  11.5 21.2 %copy-start.1 = (bf16[512,1152]{1,0:T(8,128)(2,1)S(1)}, bf16[512,1152]{1,0:T(8,128)(2,1)}, u32[]{:S(2)}) copy-start(bf16[512,1152]{1,0:T(8,128)(2,1)} %refs_0_.9) | copy-start | bytes 3538948
  28.7 15.7 %collective-permute-start.3 = (bf16[256,1152]{1,0:T(8,128)(2,1)S(1)}, bf16[256,1152]{1,0:T(8,128)(2,1)S(1)}, u32[]{:S(2)}, u32[]{:S(2)}) collective-permute-start(bf16[256,1152]{1,0:T(8,128)(2,1)S(1)} %slice.16), channel_id=1, source_target_pairs={{0,64},{1,65},{2,66},{3,67},{4,68},{5,69},{6,70},{7,71},{8,72},{9,... | collective-permute-start | bytes 1769480 | tf_op jit(solution)/shard_map/ppermute | solution.py:31
  30.3 14.2 %collective-permute-start.4 = (bf16[256,1152]{1,0:T(8,128)(2,1)S(1)}, bf16[256,1152]{1,0:T(8,128)(2,1)S(1)}, u32[]{:S(2)}, u32[]{:S(2)}) collective-permute-start(bf16[256,1152]{1,0:T(8,128)(2,1)S(1)} %slice.17), channel_id=1, source_target_pairs={{0,192},{1,193},{2,194},{3,195},{4,196},{5,197},{6,198},{7,199},{8... | collective-permute-start | bytes 1769480 | tf_op jit(solution)/shard_map/ppermute | solution.py:31
  49.6 38.4 %collective-permute-start.11 = (bf16[256,1152]{1,0:T(8,128)(2,1)S(1)}, bf16[256,1152]{1,0:T(8,128)(2,1)S(1)}, u32[]{:S(2)}, u32[]{:S(2)}) collective-permute-start(bf16[256,1152]{1,0:T(8,128)(2,1)S(1)} %get-tuple-element.71), channel_id=1, source_target_pairs={{0,32},{1,33},{2,34},{3,35},{4,36},{5,37},{6,38},{7,39},{8,40},{9,... | collective-permute-start | bytes 1769480 | tf_op jit(solution)/shard_map/ppermute | solution.py:36
  76.0 18.3 %collective-permute-start.10 = (bf16[256,1152]{1,0:T(8,128)(2,1)S(1)}, bf16[256,1152]{1,0:T(8,128)(2,1)S(1)}, u32[]{:S(2)}, u32[]{:S(2)}) collective-permute-start(bf16[256,1152]{1,0:T(8,128)(2,1)S(1)} %get-tuple-element.70), channel_id=1, source_target_pairs={{0,192},{1,193},{2,194},{3,195},{4,196},{5,197},{6,198},{7,199},{8... | collective-permute-start | bytes 1769480 | tf_op jit(solution)/shard_map/ppermute | solution.py:31
  78.0 20.0 %collective-permute-start.9 = (bf16[256,1152]{1,0:T(8,128)(2,1)S(1)}, bf16[256,1152]{1,0:T(8,128)(2,1)S(1)}, u32[]{:S(2)}, u32[]{:S(2)}) collective-permute-start(bf16[256,1152]{1,0:T(8,128)(2,1)S(1)} %get-tuple-element.65.refs_9_), channel_id=1, source_target_pairs={{0,64},{1,65},{2,66},{3,67},{4,68},{5,69},{6,70},{7,71},{8,72},{9,... | collective-permute-start | bytes 1769480 | tf_op jit(solution)/shard_map/ppermute | solution.py:31
  80.3 22.0 %collective-permute-start.6 = (bf16[256,1152]{1,0:T(8,128)(2,1)S(1)}, bf16[256,1152]{1,0:T(8,128)(2,1)S(1)}, u32[]{:S(2)}, u32[]{:S(2)}) collective-permute-start(bf16[256,1152]{1,0:T(8,128)(2,1)S(1)} %get-tuple-element.66), channel_id=1, source_target_pairs={{0,192},{1,193},{2,194},{3,195},{4,196},{5,197},{6,198},{7,199},{8... | collective-permute-start | bytes 1769480 | tf_op jit(solution)/shard_map/ppermute | solution.py:31
  81.7 20.6 %collective-permute-start.7 = (bf16[256,1152]{1,0:T(8,128)(2,1)S(1)}, bf16[256,1152]{1,0:T(8,128)(2,1)S(1)}, u32[]{:S(2)}, u32[]{:S(2)}) collective-permute-start(bf16[256,1152]{1,0:T(8,128)(2,1)S(1)} %get-tuple-element.67.refs_12_), channel_id=1, source_target_pairs={{0,64},{1,65},{2,66},{3,67},{4,68},{5,69},{6,70},{7,71},{8,72},{9,... | collective-permute-start | bytes 1769480 | tf_op jit(solution)/shard_map/ppermute | solution.py:31
  88.0 13.6 %collective-permute-start.8 = (f32[5]{0:T(128)S(1)}, f32[5]{0:T(128)S(1)}, u32[]{:S(2)}, u32[]{:S(2)}) collective-permute-start(f32[5]{0:T(128)S(1)} %get-tuple-element.69), channel_id=1, source_target_pairs={{0,32},{1,33},{2,34},{3,35},{4,36},{5,37},{6,38},{7,39},{8,40},{9,... | collective-permute-start | bytes 68 | tf_op jit(solution)/shard_map/ppermute | solution.py:36
  94.4 25.2 %collective-permute-start.14 = (bf16[256,1152]{1,0:T(8,128)(2,1)S(1)}, bf16[256,1152]{1,0:T(8,128)(2,1)S(1)}, u32[]{:S(2)}, u32[]{:S(2)}) collective-permute-start(bf16[256,1152]{1,0:T(8,128)(2,1)S(1)} %get-tuple-element.78), channel_id=1, source_target_pairs={{0,32},{1,33},{2,34},{3,35},{4,36},{5,37},{6,38},{7,39},{8,40},{9,... | collective-permute-start | bytes 1769480 | tf_op jit(solution)/shard_map/ppermute | solution.py:36
  100.2 11.4 %collective-permute-start.13 = (bf16[256,1152]{1,0:T(8,128)(2,1)S(1)}, bf16[256,1152]{1,0:T(8,128)(2,1)S(1)}, u32[]{:S(2)}, u32[]{:S(2)}) collective-permute-start(bf16[256,1152]{1,0:T(8,128)(2,1)S(1)} %get-tuple-element.76), channel_id=1, source_target_pairs={{0,192},{1,193},{2,194},{3,195},{4,196},{5,197},{6,198},{7,199},{8... | collective-permute-start | bytes 1769480 | tf_op jit(solution)/shard_map/ppermute | solution.py:31
  101.6 11.0 %collective-permute-start.12 = (bf16[256,1152]{1,0:T(8,128)(2,1)S(1)}, bf16[256,1152]{1,0:T(8,128)(2,1)S(1)}, u32[]{:S(2)}, u32[]{:S(2)}) collective-permute-start(bf16[256,1152]{1,0:T(8,128)(2,1)S(1)} %get-tuple-element.73.refs_12_), channel_id=1, source_target_pairs={{0,64},{1,65},{2,66},{3,67},{4,68},{5,69},{6,70},{7,71},{8,72},{9,... | collective-permute-start | bytes 1769480 | tf_op jit(solution)/shard_map/ppermute | solution.py:31

commit v4 on v3

--- a/solution.py
+++ b/solution.py
@@ -36,34 +36,22 @@
     return lax.ppermute(value, "dp", [(i, i ^ (1 << Z_BIT)) for i in range(count)])
 
 
-def stage_kernel(starts, *refs):
-    count = len(starts)
-    sources, targets, sems = refs[:count], refs[-1 - count : -1], refs[-1]
-    copies = [
-        pltpu.make_async_copy(
-            sources[i].at[pl.ds(starts[i], targets[i].shape[0]), :], targets[i], sems.at[i]
-        )
-        for i in range(count)
-    ]
-    for copy in copies:
-        copy.start()
-    for copy in copies:
-        copy.wait()
-
-
-def staged(parts):
-    count = len(parts)
-    return pl.pallas_call(
-        functools.partial(stage_kernel, [first for _, first, _ in parts]),
-        out_shape=[
-            jax.ShapeDtypeStruct((rows, value.shape[1]), value.dtype) for value, _, rows in parts
-        ],
-        in_specs=[ANY] * count,
-        out_specs=[VMEM] * count,
-        scratch_shapes=[pltpu.SemaphoreType.DMA((count,))],
-        compiler_params=pltpu.CompilerParams(vmem_limit_bytes=60 << 20),
+def stage_kernel(value, *halves):
+    first = 0
+    for half in halves:
+        half[...] = value[first : first + half.shape[0], :]
+        first += half.shape[0]
+
+
+def staged(value, rows):
+    return pl.pallas_call(
+        stage_kernel,
+        out_shape=[jax.ShapeDtypeStruct((r, value.shape[1]), value.dtype) for r in rows],
+        in_specs=[VMEM],
+        out_specs=[VMEM] * len(rows),
+        compiler_params=pltpu.CompilerParams(vmem_limit_bytes=8 << 20),
         cost_estimate=SMALL,
-    )(*[value for value, _, _ in parts])
+    )(value)
 
 
 def softplus_and_slope(u):
@@ -304,9 +292,7 @@
 
     far_images = [
         to_z(rows)
-        for rows in staged(
-            [(image_embeds, 0, FIRST), (image_embeds, FIRST, pair_rows - FIRST)]
-        )
+        for rows in staged(image_embeds, [FIRST, pair_rows - FIRST])
     ]
     text_below = to_x(text_embeds, 1)
     text_above = to_x(text_embeds, -1)

time: 123 us -> 123 us (level)
  local copies, waits for them, and re-layouts: 0.19 us -> 1.46 us
    unnamed x8 -> x10, local copies, waits for them, and re-layouts: 0.02 us -> 1.29 us
  transfers between devices with their start and end apart: 15 -> 15, of which waited for: 8 -> 8; matrix products, arithmetic and copies ran while one was open for 1% -> 1% of each run, Pallas kernels for 28% -> 27%
where the time goes in v4:
time: 123 us; the launch traced here: 121 us
  waiting for transfers between devices  49.6 us (40%)
  starting transfers between devices  33.3 us (27%)
  Pallas kernels  33.3 us (27%)
  between operations  2.07 us (2%)
  local copies, waits for them, and re-layouts  1.46 us (1%)
  other arithmetic  1.24 us (1%)
    ppermute x5, waiting for transfers between devices, to_z(): lax.ppermute(value, 'dp', [(i, i ^ 1 << Z_BIT) for i in range(count)])  25.3 us
    ppermute x10, waiting for transfers between devices, to_x(): lax.ppermute(value, 'dp', [(i, x_neighbour(i, hop)) for i in range(count)])  24.3 us
    ppermute x5, starting transfers between devices, to_z(): lax.ppermute(value, 'dp', [(i, i ^ 1 << Z_BIT) for i in range(count)])  21.8 us
    pallas_call x4, Pallas kernels, tiles(): pl.pallas_call(functools.partial(tiles_kernel, blocks, home, len(extra) >...  18.3 us
    ppermute x10, starting transfers between devices, to_x(): lax.ppermute(value, 'dp', [(i, x_neighbour(i, hop)) for i in range(count)])  11.5 us
    pallas_call x4, Pallas kernels, text_partials(): pl.pallas_call(functools.partial(text_kernel, len(images), [(first, rows)...  7.75 us
    pallas_call x1, Pallas kernels, image_partial(): pl.pallas_call(functools.partial(image_grad_kernel, blocks), out_shape=[j...  2.46 us
  transfers between devices with their start and end apart: 15, of which 8 were waited for; matrix products, arithmetic and copies ran while one was open for 1% of the time, Pallas kernels for 27%

profile of v4, /device:TPU:42, one launch (start us, length us, event | category | flops | bytes accessed | tf_op | source)
XLA Modules:
  0.0 120.9 jit_solution(1833836540680734228)
XLA Ops:
  0.6 1.6 %collective-permute-start.1 = (bf16[512,1152]{1,0:T(8,128)(2,1)}, bf16[512,1152]{1,0:T(8,128)(2,1)S(1)}, u32[]{:S(2)}, u32[]{:S(2)}) collective-permute-start(bf16[512,1152]{1,0:T(8,128)(2,1)} %refs_0_.7), channel_id=1, source_target_pairs={{0,64},{1,65},{2,66},{3,67},{4,68},{5,69},{6,70},{7,71},{8,72},{9,... | collective-permute-start | bytes 3538952 | tf_op jit(solution)/shard_map/ppermute | solution.py:31
  2.7 1.3 %copy-done = bf16[512,1152]{1,0:T(8,128)(2,1)S(1)} copy-done((bf16[512,1152]{1,0:T(8,128)(2,1)S(1)}, bf16[512,1152]{1,0:T(8,128)(2,1)}, u32[]{:S(2)}) %copy-start) | copy-done | bytes 1179672
  4.0 1.1 shard_map.86
  5.1 6.3 %collective-permute-start.2 = (bf16[256,1152]{1,0:T(8,128)(2,1)}, bf16[256,1152]{1,0:T(8,128)(2,1)S(1)}, u32[]{:S(2)}, u32[]{:S(2)}) collective-permute-start(bf16[256,1152]{1,0:T(8,128)(2,1)} %get-tuple-element.44), channel_id=1, source_target_pairs={{0,32},{1,33},{2,34},{3,35},{4,36},{5,37},{6,38},{7,39},{8,40},{9,... | collective-permute-start | bytes 1769480 | tf_op jit(solution)/shard_map/ppermute | solution.py:36
  11.5 17.1 %collective-permute-done.1.rest_2_.refs_2_ = bf16[512,1152]{1,0:T(8,128)(2,1)S(1)} collective-permute-done((bf16[512,1152]{1,0:T(8,128)(2,1)}, bf16[512,1152]{1,0:T(8,128)(2,1)S(1)}, u32[]{:S(2)}, u32[]{:S(2)}) %collective-permute-start.1) | collective-permute-done | bytes 1179680 | tf_op jit(solution)/shard_map/ppermute | solution.py:31
  28.7 1.6 %collective-permute-start.3 = (bf16[256,1152]{1,0:T(8,128)(2,1)S(1)}, bf16[256,1152]{1,0:T(8,128)(2,1)S(1)}, u32[]{:S(2)}, u32[]{:S(2)}) collective-permute-start(bf16[256,1152]{1,0:T(8,128)(2,1)S(1)} %slice.16), channel_id=1, source_target_pairs={{0,64},{1,65},{2,66},{3,67},{4,68},{5,69},{6,70},{7,71},{8,72},{9,... | collective-permute-start | bytes 1769480 | tf_op jit(solution)/shard_map/ppermute | solution.py:31
  30.3 0.8 collective-permute-start.4
  32.7 6.4 %shard_map.85 = (bf16[512,512]{1,0:T(8,128)(2,1)S(1)}, bf16[512,512]{1,0:T(8,128)(2,1)S(1)}, bf16[512,512]{1,0:T(8,128)(2,1)S(1)}, f32[512,1152]{1,0:T(8,128)S(1)}, f32[3]{0:T(128)S(1)}) custom-call(f32[2]{0:T(128)S(1)} %pad_maximum_fusion.scalars.after, f32[3]{0:T(128)S(1)} %bitcast.5, f32[2]{0:T(128)S(1)} %pad_maximum_fusion.scalars.after, ...), custom_call_target="tpu_custom_call" | custom-call | flops 1024 | bytes 1024 | tf_op jit(solution)/shard_map/pallas_call | solution.py:135
  39.2 5.2 %collective-permute-done.2.images.refs_1_ = bf16[256,1152]{1,0:T(8,128)(2,1)S(1)} collective-permute-done((bf16[256,1152]{1,0:T(8,128)(2,1)}, bf16[256,1152]{1,0:T(8,128)(2,1)S(1)}, u32[]{:S(2)}, u32[]{:S(2)}) %collective-permute-start.2) | collective-permute-done | bytes 589856 | tf_op jit(solution)/shard_map/ppermute | solution.py:36
  44.5 5.1 %shard_map.87 = (bf16[512,256]{1,0:T(8,128)(2,1)S(1)}, bf16[512,256]{1,0:T(8,128)(2,1)S(1)}, bf16[512,256]{1,0:T(8,128)(2,1)S(1)}, bf16[256,256]{1,0:T(8,128)(2,...) custom-call(f32[2]{0:T(128)S(1)} %pad_maximum_fusion.scalars.after, ...), custom_call_target="tpu_custom_call" | custom-call | flops 1024 | bytes 1024 | tf_op jit(solution)/shard_map/pallas_call | solution.py:135
  49.6 6.6 %collective-permute-start.11 = (bf16[256,1152]{1,0:T(8,128)(2,1)S(1)}, bf16[256,1152]{1,0:T(8,128)(2,1)S(1)}, u32[]{:S(2)}, u32[]{:S(2)}) collective-permute-start(bf16[256,1152]{1,0:T(8,128)(2,1)S(1)} %get-tuple-element.71), channel_id=1, source_target_pairs={{0,32},{1,33},{2,34},{3,35},{4,36},{5,37},{6,38},{7,39},{8,40},{9,... | collective-permute-start | bytes 1769480 | tf_op jit(solution)/shard_map/ppermute | solution.py:36
  56.2 2.8 %shard_map.88 = (bf16[256,512]{1,0:T(8,128)(2,1)S(1)}, bf16[256,512]{1,0:T(8,128)(2,1)S(1)}, f32[512,1152]{1,0:T(8,128)S(1)}, f32[2]{0:T(128)S(1)}) custom-call(f32[2]{0:T(128)S(1)} %pad_maximum_fusion.scalars.after, f32[2]{0:T(128)S(1)} %slice.12.flags, f32[5]{0:T(128)S(1)} %get-tuple-element.45.after.refs_10_, bf16[512,1152]{1,0:T(8,128)(2,1)S(1)} %copy-done.1, ...), custom_call_target="tpu_custom_call" | custom-call | flops 1024 | bytes 1024 | tf_op jit(solution)/shard_map/pallas_call | solution.py:135
  59.1 11.3 %collective-permute-done.5.images.refs_2_ = bf16[256,1152]{1,0:T(8,128)(2,1)S(1)} collective-permute-done((bf16[256,1152]{1,0:T(8,128)(2,1)}, bf16[256,1152]{1,0:T(8,128)(2,1)S(1)}, u32[]{:S(2)}, u32[]{:S(2)}) %collective-permute-start.5) | collective-permute-done | bytes 589856 | tf_op jit(solution)/shard_map/ppermute | solution.py:36
  70.4 4.0 %shard_map.89 = (bf16[512,256]{1,0:T(8,128)(2,1)S(1)}, bf16[512,256]{1,0:T(8,128)(2,1)S(1)}, bf16[512,256]{1,0:T(8,128)(2,1)S(1)}, bf16[256,256]{1,0:T(8,128)(2,...) custom-call(f32[2]{0:T(128)S(1)} %pad_maximum_fusion.scalars.after, f32[5]{0:T(128)S(1)} %broadcast_select_fusion.flags, ...), custom_call_target="tpu_custom_call" | custom-call | flops 1024 | bytes 1024 | tf_op jit(solution)/shard_map/pallas_call | solution.py:135
  74.4 1.5 %shard_map.90 = (bf16[256,1152]{1,0:T(8,128)(2,1)S(1)}, bf16[256,1152]{1,0:T(8,128)(2,1)S(1)}) custom-call(bf16[512,1152]{1,0:T(8,128)(2,1)S(1)} %copy-done.1, bf16[256,1152]{1,0:T(8,128)(2,1)S(1)} %collective-permute-done.2.images.refs_1_, bf16[256,1152]{1,0:T(8,128)(2,1)S(1)} %collective-permute-done.5.images.refs_2_, ...), custom_call_target="tpu_custom_call" | custom-call | flops 1024 | bytes 1024 | tf_op jit(solution)/shard_map/pallas_call | solution.py:208
  76.0 2.0 %collective-permute-start.10 = (bf16[256,1152]{1,0:T(8,128)(2,1)S(1)}, bf16[256,1152]{1,0:T(8,128)(2,1)S(1)}, u32[]{:S(2)}, u32[]{:S(2)}) collective-permute-start(bf16[256,1152]{1,0:T(8,128)(2,1)S(1)} %get-tuple-element.70), channel_id=1, source_target_pairs={{0,192},{1,193},{2,194},{3,195},{4,196},{5,197},{6,198},{7,199},{8... | collective-permute-start | bytes 1769480 | tf_op jit(solution)/shard_map/ppermute | solution.py:31
  78.0 0.8 collective-permute-start.9
  78.8 1.5 %shard_map.91 = (bf16[256,1152]{1,0:T(8,128)(2,1)S(1)}, bf16[256,1152]{1,0:T(8,128)(2,1)S(1)}) custom-call(bf16[512,1152]{1,0:T(8,128)(2,1)S(1)} %copy-done.1, bf16[256,1152]{1,0:T(8,128)(2,1)S(1)} %collective-permute-done.2.images.refs_1_, bf16[256,1152]{1,0:T(8,128)(2,1)S(1)} %collective-permute-done.5.images.refs_2_, ...), custom_call_target="tpu_custom_call" | custom-call | flops 1024 | bytes 1024 | tf_op jit(solution)/shard_map/pallas_call | solution.py:208
  80.3 1.3 %collective-permute-start.6 = (bf16[256,1152]{1,0:T(8,128)(2,1)S(1)}, bf16[256,1152]{1,0:T(8,128)(2,1)S(1)}, u32[]{:S(2)}, u32[]{:S(2)}) collective-permute-start(bf16[256,1152]{1,0:T(8,128)(2,1)S(1)} %get-tuple-element.66), channel_id=1, source_target_pairs={{0,192},{1,193},{2,194},{3,195},{4,196},{5,197},{6,198},{7,199},{8... | collective-permute-start | bytes 1769480 | tf_op jit(solution)/shard_map/ppermute | solution.py:31
  82.6 2.5 %shard_map.92 = (bf16[256,1152]{1,0:T(8,128)(2,1)S(1)}, f32[5]{0:T(128)S(1)}) custom-call(bf16[512,1152]{1,0:T(8,128)(2,1)S(1)} %copy-done.2, bf16[512,1152]{1,0:T(8,128)(2,1)S(1)} %collective-permute-done.rest_1_.refs_1_, bf16[512,1152]{1,0:T(8,128)(2,1)S(1)} %collective-permute-done.1.rest_2_.refs_2_, ...), custom_call_target="tpu_custom_call" | custom-call | flops 1024 | bytes 1024 | tf_op jit(solution)/shard_map/pallas_call | solution.py:168
  85.0 3.0 %collective-permute-done.11.block = bf16[256,1152]{1,0:T(8,128)(2,1)S(1)} collective-permute-done((bf16[256,1152]{1,0:T(8,128)(2,1)S(1)}, bf16[256,1152]{1,0:T(8,128)(2,1)S(1)}, u32[]{:S(2)}, u32[]{:S(2)}) %collective-permute-start.11) | collective-permute-done | bytes 589856 | tf_op jit(solution)/shard_map/ppermute | solution.py:36
  88.0 5.3 %collective-permute-start.8 = (f32[5]{0:T(128)S(1)}, f32[5]{0:T(128)S(1)}, u32[]{:S(2)}, u32[]{:S(2)}) collective-permute-start(f32[5]{0:T(128)S(1)} %get-tuple-element.69), channel_id=1, source_target_pairs={{0,32},{1,33},{2,34},{3,35},{4,36},{5,37},{6,38},{7,39},{8,40},{9,... | collective-permute-start | bytes 68 | tf_op jit(solution)/shard_map/ppermute | solution.py:36
  93.3 1.1 shard_map.93
  94.4 3.6 %collective-permute-start.14 = (bf16[256,1152]{1,0:T(8,128)(2,1)S(1)}, bf16[256,1152]{1,0:T(8,128)(2,1)S(1)}, u32[]{:S(2)}, u32[]{:S(2)}) collective-permute-start(bf16[256,1152]{1,0:T(8,128)(2,1)S(1)} %get-tuple-element.78), channel_id=1, source_target_pairs={{0,32},{1,33},{2,34},{3,35},{4,36},{5,37},{6,38},{7,39},{8,40},{9,... | collective-permute-start | bytes 1769480 | tf_op jit(solution)/shard_map/ppermute | solution.py:36
  98.0 2.2 %shard_map.94 = (bf16[256,1152]{1,0:T(8,128)(2,1)S(1)}, bf16[256,1152]{1,0:T(8,128)(2,1)S(1)}) custom-call(bf16[512,1152]{1,0:T(8,128)(2,1)S(1)} %copy-done.1, bf16[256,1152]{1,0:T(8,128)(2,1)S(1)} %collective-permute-done.2.images.refs_1_, bf16[256,1152]{1,0:T(8,128)(2,1)S(1)} %collective-permute-done.5.images.refs_2_, ...), custom_call_target="tpu_custom_call" | custom-call | flops 1024 | bytes 1024 | tf_op jit(solution)/shard_map/pallas_call | solution.py:208
  100.2 1.4 %collective-permute-start.13 = (bf16[256,1152]{1,0:T(8,128)(2,1)S(1)}, bf16[256,1152]{1,0:T(8,128)(2,1)S(1)}, u32[]{:S(2)}, u32[]{:S(2)}) collective-permute-start(bf16[256,1152]{1,0:T(8,128)(2,1)S(1)} %get-tuple-element.76), channel_id=1, source_target_pairs={{0,192},{1,193},{2,194},{3,195},{4,196},{5,197},{6,198},{7,199},{8... | collective-permute-start | bytes 1769480 | tf_op jit(solution)/shard_map/ppermute | solution.py:31
  102.3 2.5 %shard_map.95 = (f32[256,1152]{1,0:T(8,128)S(1)}, f32[256,1152]{1,0:T(8,128)S(1)}, f32[5]{0:T(128)S(1)}) custom-call(bf16[512,1152]{1,0:T(8,128)(2,1)S(1)} %copy-done.1, bf16[256,1152]{1,0:T(8,128)(2,1)S(1)} %collective-permute-done.2.images.refs_1_, bf16[256,1152]{1,0:T(8,128)(2,1)S(1)} %collective-permute-done.5.images.refs_2_, ...), custom_call_target="tpu_custom_call" | custom-call | flops 17179869184 | bytes 1048576 | tf_op jit(solution)/shard_map/pallas_call | solution.py:208
  105.6 6.0 %collective-permute-done.13.high_more = bf16[256,1152]{1,0:T(8,128)(2,1)S(1)} collective-permute-done((bf16[256,1152]{1,0:T(8,128)(2,1)S(1)}, bf16[256,1152]{1,0:T(8,128)(2,1)S(1)}, u32[]{:S(2)}, u32[]{:S(2)}) %collective-permute-start.13) | collective-permute-done | bytes 589856 | tf_op jit(solution)/shard_map/ppermute | solution.py:31
  111.5 1.1 collective-permute-done.12.low_more
  112.6 1.5 %shard_map.96 = f32[512,1152]{1,0:T(8,128)} custom-call(f32[256,1152]{1,0:T(8,128)S(1)} %get-tuple-element.74.low, f32[256,1152]{1,0:T(8,128)S(1)} %get-tuple-element.75.high, bf16[256,1152]{1,0:T(8,128)(2,1)S(1)} %collective-permute-done.12.low_more, bf16[256,1152]{1,0:T(8,128)(2,1)S(1)} %collective-permute-done.13.high_more), custom_call_target="tpu_custom_call" | custom-call | flops 1024 | bytes 1024 | tf_op jit(solution)/shard_map/pallas_call | solution.py:267
  114.1 5.7 %collective-permute-done.14.block = bf16[256,1152]{1,0:T(8,128)(2,1)S(1)} collective-permute-done((bf16[256,1152]{1,0:T(8,128)(2,1)S(1)}, bf16[256,1152]{1,0:T(8,128)(2,1)S(1)}, u32[]{:S(2)}, u32[]{:S(2)}) %collective-permute-start.14) | collective-permute-done | bytes 589856 | tf_op jit(solution)/shard_map/ppermute | solution.py:36
  119.9 1.1 shard_map.97
  (35 shorter events, 3.6 us)
Async XLA Ops:
  0.6 10.8 %copy-start.3 = (s32[5]{0:T(128)S(1)}, s32[5]{0:T(128)}, u32[]{:S(2)}) copy-start(s32[5]{0:T(128)} %constant.27.clone) | copy-start | bytes 64
  0.6 28.0 %collective-permute-start.1 = (bf16[512,1152]{1,0:T(8,128)(2,1)}, bf16[512,1152]{1,0:T(8,128)(2,1)S(1)}, u32[]{:S(2)}, u32[]{:S(2)}) collective-permute-start(bf16[512,1152]{1,0:T(8,128)(2,1)} %refs_0_.7), channel_id=1, source_target_pairs={{0,64},{1,65},{2,66},{3,67},{4,68},{5,69},{6,70},{7,71},{8,72},{9,... | collective-permute-start | bytes 3538952 | tf_op jit(solution)/shard_map/ppermute | solution.py:31
  2.2 28.0 %collective-permute-start = (bf16[512,1152]{1,0:T(8,128)(2,1)}, bf16[512,1152]{1,0:T(8,128)(2,1)S(1)}, u32[]{:S(2)}, u32[]{:S(2)}) collective-permute-start(bf16[512,1152]{1,0:T(8,128)(2,1)} %refs_0_.7), channel_id=1, source_target_pairs={{0,192},{1,193},{2,194},{3,195},{4,196},{5,197},{6,198},{7,199},{8... | collective-permute-start | bytes 3538952 | tf_op jit(solution)/shard_map/ppermute | solution.py:31
  2.7 1.3 %copy-start = (bf16[512,1152]{1,0:T(8,128)(2,1)S(1)}, bf16[512,1152]{1,0:T(8,128)(2,1)}, u32[]{:S(2)}) copy-start(bf16[512,1152]{1,0:T(8,128)(2,1)} %refs_0_.9) | copy-start | bytes 3538948
  4.0 7.4 %copy-start.4 = (s32[1,6]{1,0:T(1,128)S(1)}, s32[1,6]{1,0:T(1,128)}, u32[]{:S(2)}) copy-start(s32[1,6]{1,0:T(1,128)} %param.10) | copy-start | bytes 76
  5.1 39.3 %collective-permute-start.2 = (bf16[256,1152]{1,0:T(8,128)(2,1)}, bf16[256,1152]{1,0:T(8,128)(2,1)S(1)}, u32[]{:S(2)}, u32[]{:S(2)}) collective-permute-start(bf16[256,1152]{1,0:T(8,128)(2,1)} %get-tuple-element.44), channel_id=1, source_target_pairs={{0,32},{1,33},{2,34},{3,35},{4,36},{5,37},{6,38},{7,39},{8,40},{9,... | collective-permute-start | bytes 1769480 | tf_op jit(solution)/shard_map/ppermute | solution.py:36
  11.4 59.0 %collective-permute-start.5 = (bf16[256,1152]{1,0:T(8,128)(2,1)}, bf16[256,1152]{1,0:T(8,128)(2,1)S(1)}, u32[]{:S(2)}, u32[]{:S(2)}) collective-permute-start(bf16[256,1152]{1,0:T(8,128)(2,1)} %get-tuple-element.48), channel_id=1, source_target_pairs={{0,32},{1,33},{2,34},{3,35},{4,36},{5,37},{6,38},{7,39},{8,40},{9,... | collective-permute-start | bytes 1769480 | tf_op jit(solution)/shard_map/ppermute | solution.py:36
  11.5 21.2 %copy-start.1 = (bf16[512,1152]{1,0:T(8,128)(2,1)S(1)}, bf16[512,1152]{1,0:T(8,128)(2,1)}, u32[]{:S(2)}) copy-start(bf16[512,1152]{1,0:T(8,128)(2,1)} %refs_0_.9) | copy-start | bytes 3538948
  11.5 21.2 %copy-start.2 = (bf16[512,1152]{1,0:T(8,128)(2,1)S(1)}, bf16[512,1152]{1,0:T(8,128)(2,1)}, u32[]{:S(2)}) copy-start(bf16[512,1152]{1,0:T(8,128)(2,1)} %refs_0_.7) | copy-start | bytes 3538948
  28.7 15.7 %collective-permute-start.3 = (bf16[256,1152]{1,0:T(8,128)(2,1)S(1)}, bf16[256,1152]{1,0:T(8,128)(2,1)S(1)}, u32[]{:S(2)}, u32[]{:S(2)}) collective-permute-start(bf16[256,1152]{1,0:T(8,128)(2,1)S(1)} %slice.16), channel_id=1, source_target_pairs={{0,64},{1,65},{2,66},{3,67},{4,68},{5,69},{6,70},{7,71},{8,72},{9,... | collective-permute-start | bytes 1769480 | tf_op jit(solution)/shard_map/ppermute | solution.py:31
  30.3 14.2 %collective-permute-start.4 = (bf16[256,1152]{1,0:T(8,128)(2,1)S(1)}, bf16[256,1152]{1,0:T(8,128)(2,1)S(1)}, u32[]{:S(2)}, u32[]{:S(2)}) collective-permute-start(bf16[256,1152]{1,0:T(8,128)(2,1)S(1)} %slice.17), channel_id=1, source_target_pairs={{0,192},{1,193},{2,194},{3,195},{4,196},{5,197},{6,198},{7,199},{8... | collective-permute-start | bytes 1769480 | tf_op jit(solution)/shard_map/ppermute | solution.py:31
  49.6 38.4 %collective-permute-start.11 = (bf16[256,1152]{1,0:T(8,128)(2,1)S(1)}, bf16[256,1152]{1,0:T(8,128)(2,1)S(1)}, u32[]{:S(2)}, u32[]{:S(2)}) collective-permute-start(bf16[256,1152]{1,0:T(8,128)(2,1)S(1)} %get-tuple-element.71), channel_id=1, source_target_pairs={{0,32},{1,33},{2,34},{3,35},{4,36},{5,37},{6,38},{7,39},{8,40},{9,... | collective-permute-start | bytes 1769480 | tf_op jit(solution)/shard_map/ppermute | solution.py:36
  76.0 18.4 %collective-permute-start.10 = (bf16[256,1152]{1,0:T(8,128)(2,1)S(1)}, bf16[256,1152]{1,0:T(8,128)(2,1)S(1)}, u32[]{:S(2)}, u32[]{:S(2)}) collective-permute-start(bf16[256,1152]{1,0:T(8,128)(2,1)S(1)} %get-tuple-element.70), channel_id=1, source_target_pairs={{0,192},{1,193},{2,194},{3,195},{4,196},{5,197},{6,198},{7,199},{8... | collective-permute-start | bytes 1769480 | tf_op jit(solution)/shard_map/ppermute | solution.py:31
  78.0 20.0 %collective-permute-start.9 = (bf16[256,1152]{1,0:T(8,128)(2,1)S(1)}, bf16[256,1152]{1,0:T(8,128)(2,1)S(1)}, u32[]{:S(2)}, u32[]{:S(2)}) collective-permute-start(bf16[256,1152]{1,0:T(8,128)(2,1)S(1)} %get-tuple-element.65.refs_9_), channel_id=1, source_target_pairs={{0,64},{1,65},{2,66},{3,67},{4,68},{5,69},{6,70},{7,71},{8,72},{9,... | collective-permute-start | bytes 1769480 | tf_op jit(solution)/shard_map/ppermute | solution.py:31
  80.3 22.0 %collective-permute-start.6 = (bf16[256,1152]{1,0:T(8,128)(2,1)S(1)}, bf16[256,1152]{1,0:T(8,128)(2,1)S(1)}, u32[]{:S(2)}, u32[]{:S(2)}) collective-permute-start(bf16[256,1152]{1,0:T(8,128)(2,1)S(1)} %get-tuple-element.66), channel_id=1, source_target_pairs={{0,192},{1,193},{2,194},{3,195},{4,196},{5,197},{6,198},{7,199},{8... | collective-permute-start | bytes 1769480 | tf_op jit(solution)/shard_map/ppermute | solution.py:31
  81.6 20.7 %collective-permute-start.7 = (bf16[256,1152]{1,0:T(8,128)(2,1)S(1)}, bf16[256,1152]{1,0:T(8,128)(2,1)S(1)}, u32[]{:S(2)}, u32[]{:S(2)}) collective-permute-start(bf16[256,1152]{1,0:T(8,128)(2,1)S(1)} %get-tuple-element.67.refs_12_), channel_id=1, source_target_pairs={{0,64},{1,65},{2,66},{3,67},{4,68},{5,69},{6,70},{7,71},{8,72},{9,... | collective-permute-start | bytes 1769480 | tf_op jit(solution)/shard_map/ppermute | solution.py:31
  88.0 13.6 %collective-permute-start.8 = (f32[5]{0:T(128)S(1)}, f32[5]{0:T(128)S(1)}, u32[]{:S(2)}, u32[]{:S(2)}) collective-permute-start(f32[5]{0:T(128)S(1)} %get-tuple-element.69), channel_id=1, source_target_pairs={{0,32},{1,33},{2,34},{3,35},{4,36},{5,37},{6,38},{7,39},{8,40},{9,... | collective-permute-start | bytes 68 | tf_op jit(solution)/shard_map/ppermute | solution.py:36
  94.4 25.5 %collective-permute-start.14 = (bf16[256,1152]{1,0:T(8,128)(2,1)S(1)}, bf16[256,1152]{1,0:T(8,128)(2,1)S(1)}, u32[]{:S(2)}, u32[]{:S(2)}) collective-permute-start(bf16[256,1152]{1,0:T(8,128)(2,1)S(1)} %get-tuple-element.78), channel_id=1, source_target_pairs={{0,32},{1,33},{2,34},{3,35},{4,36},{5,37},{6,38},{7,39},{8,40},{9,... | collective-permute-start | bytes 1769480 | tf_op jit(solution)/shard_map/ppermute | solution.py:36
  100.2 11.3 %collective-permute-start.13 = (bf16[256,1152]{1,0:T(8,128)(2,1)S(1)}, bf16[256,1152]{1,0:T(8,128)(2,1)S(1)}, u32[]{:S(2)}, u32[]{:S(2)}) collective-permute-start(bf16[256,1152]{1,0:T(8,128)(2,1)S(1)} %get-tuple-element.76), channel_id=1, source_target_pairs={{0,192},{1,193},{2,194},{3,195},{4,196},{5,197},{6,198},{7,199},{8... | collective-permute-start | bytes 1769480 | tf_op jit(solution)/shard_map/ppermute | solution.py:31
  101.6 11.0 %collective-permute-start.12 = (bf16[256,1152]{1,0:T(8,128)(2,1)S(1)}, bf16[256,1152]{1,0:T(8,128)(2,1)S(1)}, u32[]{:S(2)}, u32[]{:S(2)}) collective-permute-start(bf16[256,1152]{1,0:T(8,128)(2,1)S(1)} %get-tuple-element.73.refs_12_), channel_id=1, source_target_pairs={{0,64},{1,65},{2,66},{3,67},{4,68},{5,69},{6,70},{7,71},{8,72},{9,... | collective-permute-start | bytes 1769480 | tf_op jit(solution)/shard_map/ppermute | solution.py:31
